TPU v7x, 512 devices: a whole 4x8x8 slice. The times are simulated.
512 devices in a mesh: gx: 8 (over z), gy: 8 (over y), gz: 8 (over x, core).
Axes of the slice: x: 4, y: 8, z: 8, core: 2. Of those that a mesh axis runs over, the one named last changes fastest.
Arguments:
- levels: int32 [64, 64, 1024], P('gx', 'gy', 'gz'), may hold values from 1 to 255
- residual: float32 [3, 64, 64, 1024], P(None, 'gx', 'gy', 'gz'), may hold values from -4 to 4
Outputs:
- correction: float32 [3, 64, 64, 1024], P(None, 'gx', 'gy', 'gz')
- coarse: float32 [3, 32, 32, 512], P(None, 'gx', 'gy', 'gz')
All inputs are finite; a program needn't handle non-finite values.
Results may differ from a plain program's by a relative error of at most 0.00002.
Values sent between devices are 32-bit elements; how exact they have to be, the bound alone decides.
No kernel may reach another device: no remote copies, remote signals or barrier semaphores. Data moves between devices by JAX's collectives and lax.ppermute only.
A program may use at most 128 MiB of HBM per device.

v0:
```python
import jax
import jax.numpy as jnp
from jax import lax
from jax.experimental import pallas as pl
from jax.experimental.pallas import tpu as pltpu
from jax.sharding import PartitionSpec as P

SWEEPS = 4
THETA = 1.15
DELTA = 0.85

FACE, SIDE, EDGE, FLAT, TURN, TWIST = 9.6, 6.0, 2.7, 1.8, 0.9, 0.4
UNIT = 120.0
WHOLE = 1.92
HALO = 16
CHUNKS = (4, 3, 2, 1)
FAR = pltpu.HBM


def sweep_scales():
    sigma = THETA / DELTA
    rho = 1.0 / sigma
    scales = []
    for _ in range(SWEEPS - 1):
        rho_next = 1.0 / (2.0 * sigma - rho)
        scales.append((rho_next * rho, 2.0 * rho_next / DELTA))
        rho = rho_next
    return scales


def lane_index():
    return lax.broadcasted_iota(jnp.int32, (8, 128), 1)


def by_group(values):
    group = lane_index() // 32
    out = jnp.full((8, 128), values[-1], jnp.float32)
    for g in range(len(values) - 1):
        out = jnp.where(group == g, values[g], out)
    return out


def neighbourhood(load, count):
    mid, summed, spread = [], [], []
    for p in range(-1, count + 1):
        u, yp, ym = load(p, 0), load(p, 1), load(p, -1)
        mid.append(u)
        summed.append(yp + ym)
        spread.append(yp - ym)
    return mid, summed, spread


def stencil(field, plane, count, row):
    def loader(c):
        return lambda p, dy: field[c, plane + p, pl.ds(row + dy, 8), :]

    flat, even, odd = ([[None] * 3 for _ in range(count)] for _ in range(3))
    cross, along, across = [None] * count, [None] * count, [None] * count
    mid, summed, spread = neighbourhood(loader(0), count)
    for p in range(count):
        u, sy = mid[p + 1], summed[p + 1]
        sx, sxy = mid[p + 2] + mid[p], summed[p + 2] + summed[p]
        flat[p][0] = FACE * sx + SIDE * sy + EDGE * sxy
        even[p][0] = SIDE * u + EDGE * sx + FLAT * sy + sxy
        cross[p] = spread[p + 2] - spread[p]
        along[p], across[p] = mid[p + 2] - mid[p], summed[p + 2] - summed[p]
    mid, summed, spread = neighbourhood(loader(1), count)
    for p in range(count):
        u, sy = mid[p + 1], summed[p + 1]
        sx, sxy = mid[p + 2] + mid[p], summed[p + 2] + summed[p]
        flat[p][1] = FACE * sy + SIDE * sx + EDGE * sxy + TURN * cross[p]
        even[p][1] = SIDE * u + EDGE * sy + FLAT * sx + sxy + TWIST * cross[p]
        back = spread[p + 2] - spread[p]
        flat[p][0] = flat[p][0] + TURN * back
        even[p][0] = even[p][0] + TWIST * back
        odd[p][2] = TURN * (along[p] + spread[p + 1]) + TWIST * (across[p] + (spread[p + 2] + spread[p]))
    mid, summed, spread = neighbourhood(loader(2), count)
    for p in range(count):
        both, sxy = mid[p + 2] + mid[p] + summed[p + 1], summed[p + 2] + summed[p]
        flat[p][2] = SIDE * both + FLAT * sxy
        even[p][2] = FACE * mid[p + 1] + EDGE * both + sxy
        odd[p][0] = TURN * (mid[p + 2] - mid[p]) + TWIST * (summed[p + 2] - summed[p])
        odd[p][1] = TURN * spread[p + 1] + TWIST * (spread[p + 2] + spread[p])
    return [[(flat[p][c], even[p][c] + odd[p][c], even[p][c] - odd[p][c]) for c in range(3)] for p in range(count)]


def side_stencil(field, plane, count, row):
    mid, summed, spread = neighbourhood(lambda p, dy: field[plane + p, pl.ds(row + dy, 8), :], count)
    group = lane_index() // 32
    flat_x, flat_y = by_group((FACE, SIDE, SIDE)), by_group((SIDE, FACE, SIDE))
    flat_xy, even_u = by_group((EDGE, EDGE, FLAT)), by_group((SIDE, SIDE, FACE))
    even_x, even_y = by_group((EDGE, FLAT, EDGE)), by_group((FLAT, EDGE, EDGE))
    found = []
    for p in range(count):
        u, sy, dy = mid[p + 1], summed[p + 1], spread[p + 1]
        sx, dx = mid[p + 2] + mid[p], mid[p + 2] - mid[p]
        sxy, dx_sy = summed[p + 2] + summed[p], summed[p + 2] - summed[p]
        dy_sx, dxy = spread[p + 2] + spread[p], spread[p + 2] - spread[p]
        along_x, along_y = TURN * dx + TWIST * dx_sy, TURN * dy + TWIST * dy_sx
        down = pltpu.roll(jnp.where(group == 1, dxy, along_y), 96, 1)
        up = pltpu.roll(jnp.where(group == 0, dxy, along_y), 32, 1)
        far = pltpu.roll(along_x, 64, 1)
        cross = jnp.where(group == 0, down, jnp.where(group == 1, up, 0.0))
        flat = flat_x * sx + flat_y * sy + flat_xy * sxy + TURN * cross
        even = even_u * u + even_x * sx + even_y * sy + sxy + TWIST * cross
        odd = jnp.where(group == 0, far, jnp.where(group == 1, down, far + up))
        found.append((flat, even + odd, even - odd))
    return found


def join_ring(part):
    centre, above, below = part
    return centre + (pltpu.roll(above, 127, 1) + pltpu.roll(below, 1, 1))


def side_lanes():
    lane = lane_index()
    return lane, lane % 32 == HALO


def join_sides(parts, side):
    lane, begins = side_lanes()
    ends = jnp.where(begins, side[1], side[2])
    side_above, side_below = side[1], side[2]
    joined = []
    for c, (centre, above, below) in enumerate(parts):
        inward = pltpu.roll(ends, 112 - 32 * c, 1)
        outward = pltpu.roll(jnp.where(lane == 0, above, below), 32 * c + HALO, 1)
        up = pltpu.roll(jnp.where(lane == 0, inward, above), 127, 1)
        down = pltpu.roll(jnp.where(lane == 127, inward, below), 1, 1)
        joined.append(centre + (up + down))
        side_above = jnp.where(lane == 32 * c + HALO, outward, side_above)
        side_below = jnp.where(lane == 32 * c + HALO - 1, outward, side_below)
    return joined, side[0] + (pltpu.roll(side_above, 127, 1) + pltpu.roll(side_below, 1, 1))


def shifted(main, side):
    lane, begins = side_lanes()
    inward = pltpu.roll(side, 112, 1)
    side_below, side_above = side, side
    for g in range(4):
        outward = pltpu.roll(main, 32 * g + HALO, 1)
        side_above = jnp.where(lane == 32 * g + HALO, outward, side_above)
        side_below = jnp.where(lane == 32 * g + HALO - 1, outward, side_below)
    return (
        (pltpu.roll(jnp.where(lane == 127, inward, main), 1, 1), pltpu.roll(jnp.where(lane == 0, inward, main), 127, 1)),
        (pltpu.roll(side_below, 1, 1), pltpu.roll(side_above, 127, 1)),
    )


def weighted(modulus, plain, heavy):
    here, before, after = modulus
    return (here * plain[0] + heavy[0], before * plain[1] + heavy[1], after * plain[2] + heavy[2])


def coupling(now, modulus, plane, count, row):
    plain, heavy = (stencil(now[k], plane, count, row) for k in range(2))
    parts = [[weighted(modulus[p][0], *both) for both in zip(plain[p], heavy[p])] for p in range(count)]
    if len(now) == 2:
        return [([join_ring(part) for part in parts[p]], None) for p in range(count)]
    plain, heavy = (side_stencil(now[2 + k], plane, count, row) for k in range(2))
    return [join_sides(parts[p], weighted(modulus[p][1], plain[p], heavy[p])) for p in range(count)]


def sweep(planes, rows, now, later, rest, modulus, diag, inverse, scale, emit=None):
    lo, hi = planes
    chunk = next(n for n in CHUNKS if (hi - lo) % n == 0)
    sides = len(rest) if not emit else 1

    def body(i, carry):
        first = lo + i * chunk
        for row in rows:
            mods = [[[read(first + j, row) for read in reads] for reads in modulus] for j in range(chunk)]
            out = coupling(now, mods, first, chunk, 8 + row)
            for j in range(chunk):
                plane = first + j
                for t in range(sides):
                    d = diag[t](plane, row)
                    if scale:
                        inv = inverse[t](plane, row) * scale[1]
                    for c in range(1 if t else 3):
                        at = (plane,) if t else (c, plane)
                        here, margin = (*at, pl.ds(row, 8), slice(None)), (*at, pl.ds(8 + row, 8), slice(None))
                        old = now[2 * t][margin]
                        r = rest[t][here] - d * old + (out[j][1] if t else out[j][0][c])
                        if not emit:
                            rest[t][here] = r
                        if scale:
                            step = inv * r
                            if scale[0]:
                                step = scale[0] * old + step
                            if emit:
                                emit(c, plane, step)
                            else:
                                later[2 * t][margin] = step
                                later[2 * t + 1][margin] = mods[j][t][0] * step
        return carry

    lax.fori_loop(0, (hi - lo) // chunk, body, 0)


def diagonal_parts(modulus, plane, row):
    def at(dx, dy):
        return modulus[plane + dx, pl.ds(row + dy, 8), :]

    u = at(0, 0)
    cross = (at(1, 0) + at(-1, 0)) + (at(0, 1) + at(0, -1))
    corner = (at(1, 1) + at(-1, -1)) + (at(1, -1) + at(-1, 1))
    even = 0.16 * u + 0.06 * cross + 0.03 * corner
    return u, (WHOLE * u + 0.16 * cross + 0.06 * corner, even, even)


def finish_diagonal(mid, total):
    diag = (1.05 * 0.5 * UNIT) * total
    inside = mid > 0.0
    return mid, diag, jnp.where(inside, 1.0 / jnp.where(inside, diag, 1.0), 0.0)


def ring_diagonal(modulus, plane, row):
    mid, part = diagonal_parts(modulus, plane, row)
    return finish_diagonal(mid, join_ring(part))


def side_diagonal(modulus, side_modulus, plane, row):
    mid, (centre, even, _) = diagonal_parts(modulus, plane, row)
    side_mid, (side_centre, side_even, _) = diagonal_parts(side_modulus, plane, row)
    (below, above), (side_below, side_above) = shifted(even, side_even)
    main = finish_diagonal(mid, centre + (below + above))
    side_mid, side_diag, side_inverse = finish_diagonal(side_mid, side_centre + (side_below + side_above))
    side_inverse = jnp.where(lane_index() < 96, side_inverse, 0.0)
    return main, (side_mid, side_diag, side_inverse), shifted(mid, side_mid)


def pair_matrix(group, fine_axis):
    fine = lax.broadcasted_iota(jnp.int32, (128, 128), fine_axis)
    coarse = lax.broadcasted_iota(jnp.int32, (128, 128), 1 - fine_axis)
    if group is None:
        return (lax.shift_right_logical(fine, 1) == coarse).astype(jnp.float32)
    inner = fine - 32 * group
    target = lax.shift_right_logical(fine, 1) - 16 * group + jnp.where(inner < HALO, 120, 56)
    return ((target == coarse) & (inner >= 0) & (inner < 32)).astype(jnp.float32)


def exact_dot(a, b):
    return jnp.dot(a, b, precision=lax.Precision.HIGHEST, preferred_element_type=jnp.float32)


def prepare(levels, residual, own, ahead, behind, held_levels, held_residual, sems):
    copies = [
        pltpu.make_async_copy(levels, held_levels, sems.at[0]),
        pltpu.make_async_copy(residual, held_residual, sems.at[1]),
    ]
    for copy in copies:
        copy.start()
    copies[0].wait()
    for p in range(8):
        ratio = held_levels[p].astype(jnp.float32) / 255.0
        value = (0.05 + 0.95 * ratio * ratio * ratio) / UNIT
        own[3, p] = value
        if p > 0:
            ahead[p - 1] = value
        if p < 7:
            behind[p] = value
    copies[1].wait()
    for c in range(3):
        for p in range(8):
            value = held_residual[c, p]
            own[c, p] = value
            if p > 1:
                ahead[7 + 6 * c + p - 2] = value
            if p < 6:
                behind[7 + 6 * c + p] = value


def fine_planes(own, left, right):
    found = []
    for plane in range(1, 23):
        if plane < 8:
            found.append((3, plane, left, (plane - 1,)))
        elif plane < 16:
            found.append((3, plane, own, (3, plane - 8)))
        else:
            found.append((3, plane, right, (plane - 16,)))
    for c in range(3):
        for plane in range(2, 22):
            if plane < 8:
                found.append((c, plane, left, (7 + 6 * c + plane - 2,)))
            elif plane < 16:
                found.append((c, plane, own, (c, plane - 8)))
            else:
                found.append((c, plane, right, (7 + 6 * c + plane - 16,)))
    return found


FINE_ROWS = 520


def fine_rows(c, plane):
    return (7 * (plane - 1), 7) if c == 3 else (154 + 6 * (20 * c + plane - 2), 6)


def pack_rows(own, left, right, ahead, behind):
    empty = jnp.zeros((8, 128), jnp.float32)
    ahead[pl.ds(FINE_ROWS - 8, 8), :] = empty
    behind[pl.ds(FINE_ROWS - 8, 8), :] = empty
    for c, plane, source, index in fine_planes(own, left, right):
        base, count = fine_rows(c, plane)
        ahead[pl.ds(base, count), :] = source[(*index, pl.ds(8 - count, count), slice(None))]
        behind[pl.ds(base, count), :] = source[(*index, pl.ds(0, count), slice(None))]


def pack_lanes(own, left, right, down, up, main, first, last):
    empty = jnp.zeros((24, 128), jnp.float32)
    for plane in (0, 1, 22, 23):
        for c in range(3):
            main[c, plane] = empty
    main[3, 0] = empty
    main[3, 23] = empty
    gap = jnp.zeros((2, 128), jnp.float32)
    for c, plane, source, index in fine_planes(own, left, right):
        base, count = fine_rows(c, plane)
        main[c, plane, pl.ds(0, 2), :] = gap
        main[c, plane, pl.ds(22, 2), :] = gap
        main[c, plane, pl.ds(8, 8), :] = source[index]
        main[c, plane, pl.ds(8 - count, count), :] = down[pl.ds(base, count), :]
        main[c, plane, pl.ds(16, count), :] = up[pl.ds(base, count), :]
    lane = lane_index()

    def pack(pair, carry):
        for t in range(3):
            head = jnp.zeros((8, 128), jnp.float32)
            tail = head
            for s in range(2):
                for c in range(4):
                    value, place = main[c, 2 * pair + s, pl.ds(8 * t, 8), :], 32 * c + HALO * s
                    mine = (lane >= place) & (lane < place + HALO)
                    head = jnp.where(mine, pltpu.roll(value, place, 1) if place else value, head)
                    turn = (place + HALO) % 128
                    tail = jnp.where(mine, pltpu.roll(value, turn, 1) if turn else value, tail)
            first[pair, pl.ds(8 * t, 8), :] = head
            last[pair, pl.ds(8 * t, 8), :] = tail
        return carry

    lax.fori_loop(0, 12, pack, 0, unroll=2)


LAYER_X = 6 * 8 + 3 * 5 * 6
LAYER_Y = 16 * 6 + 3 * 14 * 5
COARSE_ROWS_X = 192
COARSE_ROWS_Y = 368


def coarse_planes(own, left, right):
    found = []
    for i in range(16):
        if i < 6:
            found.append((3, i, left, (), 8 * i))
        elif i < 10:
            found.append((3, i, own, (3, i - 4), 0))
        else:
            found.append((3, i, right, (), 8 * (i - 10)))
    for c in range(3):
        for i in range(14):
            if i < 5:
                found.append((c, i + 1, left, (), 48 + 6 * (5 * c + i)))
            elif i < 9:
                found.append((c, i + 1, own, (c, i - 3), 1))
            else:
                found.append((c, i + 1, right, (), 48 + 6 * (5 * c + i - 9)))
    return found


def coarse_rows(c, plane):
    return (6 * plane, 6, 2) if c == 3 else (96 + 5 * (14 * c + plane - 1), 5, 1)


def pack_coarse(own, left, right, layer_ahead, layer_behind, ahead, behind):
    empty = jnp.zeros((8, 128), jnp.float32)
    for message, layer, offset in ((ahead, layer_ahead, 7), (behind, layer_behind, 4)):
        message[pl.ds(COARSE_ROWS_Y - 8, 8), :] = empty
        for f in range(4):
            base = LAYER_Y + 14 * f
            message[pl.ds(base, 1), :] = left[pl.ds(LAYER_X + 12 * f + offset, 1), :]
            message[pl.ds(base + 1, 12), :] = layer[f]
            message[pl.ds(base + 13, 1), :] = right[pl.ds(LAYER_X + 12 * f + offset, 1), :]
    for c, plane, source, index, row in coarse_planes(own, left, right):
        base, count, margin = coarse_rows(c, plane)
        ahead[pl.ds(base, count), :] = source[(*index, pl.ds(row, count), slice(None))]
        behind[pl.ds(base, count), :] = source[(*index, pl.ds(row + margin, count), slice(None))]


def smooth_kernel(
    main, before, after, smooth, message, ahead, behind, layer_ahead, layer_behind, state, side_state,
    ua, ub, va, vb, usa, usb, vsa, vsb, rest, modulus, diag, inverse, prev, next, rest_s, modulus_s, diag_s, inverse_s, prev_s, next_s, pairs, pairs_s,
):
    group = lane_index() // 32

    low = lane_index() % 32 < HALO

    def place(pair, carry):
        for s in range(2):
            plane = 2 * pair + s
            for t in range(3):
                here = pl.ds(8 * t, 8)
                for c in range(3):
                    rest[c, plane, here, :] = main[c, plane, here, :]
                modulus[plane, pl.ds(8 + 8 * t, 8), :] = main[3, plane, here, :]
                lower, upper = before[pair, here, :], after[pair, here, :]
                if s:
                    lower = pltpu.roll(lower, 128 - HALO, 1)
                else:
                    upper = pltpu.roll(upper, HALO, 1)
                value = jnp.where(low, lower, upper)
                rest_s[plane, here, :] = value
                spread = jnp.where(group == 1, pltpu.roll(value, 64, 1), pltpu.roll(value, 96, 1))
                spread = jnp.where(group == 0, pltpu.roll(value, 32, 1), spread)
                modulus_s[plane, pl.ds(8 + 8 * t, 8), :] = jnp.where(group == 3, value, spread)
        return carry

    lax.fori_loop(0, 12, place, 0, unroll=2)

    def begin(i, carry):
        for plane in (2 + 2 * i, 3 + 2 * i):
            for t in range(3):
                here, margin = pl.ds(8 * t, 8), pl.ds(8 + 8 * t, 8)
                (mid, d, inv), (mid_s, d_s, inv_s), beside = side_diagonal(modulus, modulus_s, plane, 8 + 8 * t)
                for refs, values in zip(((prev, next), (prev_s, next_s)), beside):
                    for ref, value in zip(refs, values):
                        ref[plane, here, :] = value
                diag[plane, here, :] = d
                inverse[plane, here, :] = inv
                diag_s[plane, here, :] = d_s
                inverse_s[plane, here, :] = inv_s
                inv = inv * (1.0 / THETA)
                for c in range(3):
                    step = rest[c, plane, here, :] * inv
                    ua[c, plane, margin, :] = step
                    va[c, plane, margin, :] = mid * step
                step = rest_s[plane, here, :] * (inv_s * (1.0 / THETA))
                usa[plane, margin, :] = step
                vsa[plane, margin, :] = mid_s * step
        return carry

    lax.fori_loop(0, 10, begin, 0)

    def gather(steps, start):
        def body(p, carry):
            for c in range(3):
                step = steps[c, 8 + p, pl.ds(16, 8), :]
                smooth[c, p] = step if start else smooth[c, p] + step
            return carry

        lax.fori_loop(0, 8, body, 0, unroll=4)

    gather(ua, True)
    scales = sweep_scales()

    def reader(ref, margin):
        return lambda plane, row: ref[plane, pl.ds(margin + row, 8), :]

    moduli = [
        [reader(modulus, 8), reader(prev, 0), reader(next, 0)],
        [reader(modulus_s, 8), reader(prev_s, 0), reader(next_s, 0)],
    ]
    readers = [moduli] + [[reader(ref, 0) for ref in refs] for refs in ((diag, diag_s), (inverse, inverse_s))]
    for k in range(1, SWEEPS + 1):
        now, later = (ua, va, usa, vsa), (ub, vb, usb, vsb)
        if k % 2 == 0:
            now, later = later, now
        rows = (0, 8, 16) if k == 1 else (4, 12)
        sweep((2 + k, 22 - k), rows, now, later, (rest, rest_s), *readers, scales[k - 1] if k < SWEEPS else None)
        if k < SWEEPS:
            gather(later[0], False)

    def restrict(p, carry):
        def four(ref, at, margin):
            a, b = (ref[(*at, 4 + 2 * p + dx, pl.ds(margin + 4, 8, stride=2), slice(None))] for dx in range(2))
            c, d = (ref[(*at, 4 + 2 * p + dx, pl.ds(margin + 5, 8, stride=2), slice(None))] for dx in range(2))
            return (a + b) + (c + d)

        for c in range(3):
            pairs[c, p] = four(rest, (c,), 0)
        pairs[3, p] = 0.25 * four(modulus, (), 8)
        pairs_s[0, p] = four(rest_s, (), 0)
        pairs_s[1, p] = 0.25 * four(modulus_s, (), 8)
        return carry

    lax.fori_loop(0, 8, restrict, 0, unroll=2)
    coarse = exact_dot(pairs[...].reshape(256, 128), pair_matrix(None, 0)).reshape(4, 8, 8, 128)
    for c in range(4):
        source = pairs_s[1 if c == 3 else 0].reshape(64, 128)
        message[c] = coarse[c] + exact_dot(source, pair_matrix(c % 3, 0)).reshape(8, 8, 128)
    for i in range(6):
        ahead[pl.ds(8 * i, 8), :] = message[3, i]
        behind[pl.ds(8 * i, 8), :] = message[3, 2 + i]
    for f, source in enumerate([rest.at[c] for c in range(3)] + [rest_s]):
        ahead[pl.ds(LAYER_X + 12 * f, 12), :] = source[13, pl.ds(6, 12), :]
        behind[pl.ds(LAYER_X + 12 * f, 12), :] = source[10, pl.ds(6, 12), :]
        for p in range(12):
            layer_ahead[f, pl.ds(p, 1), :] = source[6 + p, pl.ds(13, 1), :]
            layer_behind[f, pl.ds(p, 1), :] = source[6 + p, pl.ds(10, 1), :]
    empty = jnp.zeros((6, 128), jnp.float32)
    ahead[pl.ds(LAYER_X + 48, 6), :] = empty
    behind[pl.ds(LAYER_X + 48, 6), :] = empty
    for c in range(3):
        for i in range(5):
            ahead[pl.ds(48 + 6 * (5 * c + i), 6), :] = message[c, 1 + i, pl.ds(1, 6), :]
            behind[pl.ds(48 + 6 * (5 * c + i), 6), :] = message[c, 2 + i, pl.ds(1, 6), :]

    kept = (
        (modulus, modulus_s, 12), (diag, diag_s, 4), (inverse, inverse_s, 4), (prev, prev_s, 4), (next, next_s, 4)
    )

    def keep_state(p, carry):
        for c in range(3):
            state[c, p] = rest[c, 4 + p, pl.ds(4, 16), :]
        side_state[0, p] = rest_s[4 + p, pl.ds(4, 16), :]
        for f, (ref, ref_s, row) in enumerate(kept):
            state[3 + f, p] = ref[4 + p, pl.ds(row, 16), :]
            side_state[1 + f, p] = ref_s[4 + p, pl.ds(row, 16), :]
        return carry

    lax.fori_loop(0, 16, keep_state, 0, unroll=2)


def post_kernel(
    own, left, right, down, up, state_in, side_in, smooth, correction, coarse,
    ca, cb, cva, cvb, crest, cmod, cinv, cdiag, cprev, cnext, total, ua, ub, va, vb, usa, usb, vsa, vsb, wide, wide_s, rest, rest_s,
):
    scales = sweep_scales()

    empty = jnp.zeros((16, 128), jnp.float32)
    for c in range(3):
        crest[c, 0] = empty
        crest[c, 15] = empty
    edge = jnp.zeros((1, 128), jnp.float32)
    for c, plane, source, index, row in coarse_planes(own, left, right):
        base, count, margin = coarse_rows(c, plane)
        mid = source[(*index, pl.ds(row + margin, 4), slice(None))]
        below, above = down[pl.ds(base, count), :], up[pl.ds(base, count), :]
        if c < 3:
            crest[c, plane, pl.ds(0, 1), :] = edge
            crest[c, plane, pl.ds(1, 5), :] = below
            crest[c, plane, pl.ds(6, 4), :] = mid
            crest[c, plane, pl.ds(10, 5), :] = above
            crest[c, plane, pl.ds(15, 1), :] = edge
        else:
            cmod[plane, pl.ds(8, 6), :] = below
            cmod[plane, pl.ds(14, 4), :] = mid
            cmod[plane, pl.ds(18, 6), :] = above

    def begin(i, carry):
        for plane in (1 + 2 * i, 2 + 2 * i):
            for t in range(2):
                here, margin = pl.ds(8 * t, 8), pl.ds(8 + 8 * t, 8)
                mid, d, inv = ring_diagonal(cmod, plane, 8 + 8 * t)
                cdiag[plane, here, :] = d
                cprev[plane, here, :] = pltpu.roll(mid, 1, 1)
                cnext[plane, here, :] = pltpu.roll(mid, 127, 1)
                cinv[plane, here, :] = inv
                inv = inv * (1.0 / THETA)
                for c in range(3):
                    step = crest[c, plane, here, :] * inv
                    ca[c, plane, margin, :] = step
                    cva[c, plane, margin, :] = mid * step
        return carry

    lax.fori_loop(0, 7, begin, 0)

    def gather(steps, start):
        def body(p, carry):
            for c in range(3):
                step = steps[c, 4 + p, pl.ds(12, 8), :]
                total[c, p] = step if start else total[c, p] + step
            return carry

        lax.fori_loop(0, 8, body, 0, unroll=4)

    gather(ca, True)

    def reader(ref, margin):
        return lambda plane, row: ref[plane, pl.ds(margin + row, 8), :]

    coarse_moduli = [[reader(cmod, 8), reader(cprev, 0), reader(cnext, 0)]]
    for k in range(1, SWEEPS):
        now, later = ((ca, cva), (cb, cvb)) if k % 2 else ((cb, cvb), (ca, cva))
        sweep((1 + k, 15 - k), (0, 8), now, later, (crest,), coarse_moduli, [reader(cdiag, 0)], [reader(cinv, 0)], scales[k - 1])
        gather(later[0], False)

    for c in range(3):
        for p in range(4):
            coarse[c, p] = total[c, 2 + p, pl.ds(2, 4), pl.ds(0, 64)]

    wide[...] = exact_dot(total[...].reshape(192, 128), pair_matrix(None, 1)).reshape(3, 8, 8, 128)
    spread = None
    for c in range(3):
        part = exact_dot(total[c].reshape(64, 128), pair_matrix(c, 1))
        spread = part if spread is None else spread + part
    wide_s[...] = spread.reshape(8, 8, 128)

    def lift(p, carry):
        for dx in range(2):
            for dy in range(2):
                for c in range(3):
                    ua[c, 2 * p + dx, pl.ds(8 + dy, 8, stride=2), :] = wide[c, p]
                usa[2 * p + dx, pl.ds(8 + dy, 8, stride=2), :] = wide_s[p]
        return carry

    lax.fori_loop(0, 8, lift, 0, unroll=2)

    def weigh(p, carry):
        for c in range(3):
            va[c, p, pl.ds(8, 16), :] = state_in[3, p] * ua[c, p, pl.ds(8, 16), :]
            rest[c, p] = state_in[c, p]
        vsa[p, pl.ds(8, 16), :] = side_in[1, p] * usa[p, pl.ds(8, 16), :]
        rest_s[p] = side_in[0, p]
        return carry

    lax.fori_loop(0, 16, weigh, 0, unroll=2)
    for f, target in enumerate([rest.at[c] for c in range(3)] + [rest_s]):
        target[1, pl.ds(2, 12), :] = left[pl.ds(LAYER_X + 12 * f, 12), :]
        target[14, pl.ds(2, 12), :] = right[pl.ds(LAYER_X + 12 * f, 12), :]
        for p in range(14):
            target[1 + p, pl.ds(1, 1), :] = down[pl.ds(LAYER_Y + 14 * f + p, 1), :]
            target[1 + p, pl.ds(14, 1), :] = up[pl.ds(LAYER_Y + 14 * f + p, 1), :]

    def add_own(steps, start):
        def body(p, carry):
            for c in range(3):
                step = steps[c, 4 + p, pl.ds(12, 8), :]
                correction[c, p] = (smooth[c, p] if start else correction[c, p]) + step
            return carry

        lax.fori_loop(0, 8, body, 0, unroll=4)

    add_own(ua, True)

    def held(f):
        return [
            lambda plane, row: state_in[3 + f, plane, pl.ds(row, 8), :],
            lambda plane, row: side_in[1 + f, plane, pl.ds(row, 8), :],
        ]

    moduli = list(zip(held(0), held(3), held(4)))

    def emit(c, plane, step):
        correction[c, plane - 4] = correction[c, plane - 4] + step

    for k in range(SWEEPS):
        now, later = (ua, va, usa, vsa), (ub, vb, usb, vsb)
        if k % 2:
            now, later = later, now
        scale = scales[k - 1] if k else (None, 1.0 / THETA)
        last = k == SWEEPS - 1
        sweep(
            (1 + k, 15 - k), (4,) if last else (0, 8), now, later, (rest, rest_s), moduli, held(1), held(2), scale,
            emit if last else None,
        )
        if not last:
            add_own(later[0], False)


def call(kernel, outs, scratch=(), far=False, extra=()):
    return pl.pallas_call(
        kernel,
        out_shape=[jax.ShapeDtypeStruct(s, jnp.float32) for s in outs],
        **(dict(in_specs=[pl.BlockSpec(memory_space=FAR)] * 2) if far else {}),
        scratch_shapes=[pltpu.VMEM(s, jnp.float32) for s in scratch] + list(extra),
        compiler_params=pltpu.CompilerParams(vmem_limit_bytes=48 * 1024 * 1024),
    )


def neighbours(to_next, to_previous, axis):
    count = lax.axis_size(axis)
    before = lax.ppermute(to_next, axis, [(i, i + 1) for i in range(count - 1)])
    after = lax.ppermute(to_previous, axis, [(i + 1, i) for i in range(count - 1)])
    return before, after


SMOOTH_OUTS = [
    (3, 8, 8, 128),
    (4, 8, 8, 128),
    (COARSE_ROWS_X, 128),
    (COARSE_ROWS_X, 128),
    (4, 12, 128),
    (4, 12, 128),
    (8, 16, 16, 128),
    (6, 16, 16, 128),
]
SMOOTH_SCRATCH = [
    *[(3, 24, 40, 128)] * 4,
    *[(24, 40, 128)] * 4,
    (3, 24, 24, 128),
    (24, 40, 128),
    *[(24, 24, 128)] * 5,
    (24, 40, 128),
    *[(24, 24, 128)] * 4,
    (4, 8, 8, 128),
    (2, 8, 8, 128),
]
POST_OUTS = [(3, 8, 8, 128), (3, 4, 4, 64)]
POST_SCRATCH = [
    *[(3, 16, 32, 128)] * 4,
    (3, 16, 16, 128),
    (16, 32, 128),
    *[(16, 16, 128)] * 4,
    (3, 8, 8, 128),
    *[(3, 16, 32, 128)] * 4,
    *[(16, 32, 128)] * 4,
    (3, 8, 8, 128),
    (8, 8, 128),
    (3, 16, 16, 128),
    (16, 16, 128),
]


def on_device(levels, residual):
    own, ahead, behind = call(
        prepare,
        [(4, 8, 8, 128), (25, 8, 128), (25, 8, 128)],
        far=True,
        extra=[pltpu.VMEM((8, 8, 128), jnp.int32), pltpu.VMEM((3, 8, 8, 128), jnp.float32), pltpu.SemaphoreType.DMA((2,))],
    )(levels, residual)
    left, right = neighbours(ahead, behind, "gx")
    ahead, behind = call(pack_rows, [(FINE_ROWS, 128)] * 2)(own, left, right)
    down, up = neighbours(ahead, behind, "gy")
    main, first, last = call(pack_lanes, [(4, 24, 24, 128), (12, 24, 128), (12, 24, 128)])(own, left, right, down, up)
    before, after = neighbours(last, first, "gz")
    smooth, own, ahead, behind, layer_ahead, layer_behind, state, side_state = call(
        smooth_kernel, SMOOTH_OUTS, SMOOTH_SCRATCH
    )(main, before, after)
    left, right = neighbours(ahead, behind, "gx")
    ahead, behind = call(pack_coarse, [(COARSE_ROWS_Y, 128)] * 2)(own, left, right, layer_ahead, layer_behind)
    down, up = neighbours(ahead, behind, "gy")
    correction, coarse = call(post_kernel, POST_OUTS, POST_SCRATCH)(own, left, right, down, up, state, side_state, smooth)
    return correction, coarse


def solution(mesh):
    return jax.shard_map(
        on_device,
        mesh=mesh,
        in_specs=(P("gx", "gy", "gz"), P(None, "gx", "gy", "gz")),
        out_specs=(P(None, "gx", "gy", "gz"), P(None, "gx", "gy", "gz")),
        check_vma=False,
    )
```

profile of v0, /device:TPU:84, one launch (start us, length us, event | category | flops | bytes accessed | tf_op | source)
XLA Modules:
  0.0 85.7 jit_solution(1695927289144066153)
XLA Ops:
  0.6 0.9 %copy-done = f32[3,8,8,128]{3,2,1,0:T(8,128)S(1)} copy-done((f32[3,8,8,128]{3,2,1,0:T(8,128)S(1)}, f32[3,8,8,128]{3,2,1,0:T(8,128)}, u32[]{:S(2)}) %copy-start) | copy-done | bytes 98328
  1.5 0.8 copy-done.1
  2.5 4.3 %collective-permute-start = (f32[25,8,128]{2,1,0:T(8,128)S(1)}, f32[25,8,128]{2,1,0:T(8,128)S(1)}, u32[]{:S(2)}, u32[]{:S(2)}) collective-permute-start(f32[25,8,128]{2,1,0:T(8,128)S(1)} %get-tuple-element.21), channel_id=1, source_target_pairs={{0,64},{64,128},{128,192},{192,256},{256,320},{320,384},{384,448},... | collective-permute-start | bytes 307208 | tf_op jit(solution)/shard_map/ppermute | solution.py:675
  6.8 1.9 %collective-permute-start.1 = (f32[25,8,128]{2,1,0:T(8,128)S(1)}, f32[25,8,128]{2,1,0:T(8,128)S(1)}, u32[]{:S(2)}, u32[]{:S(2)}) collective-permute-start(f32[25,8,128]{2,1,0:T(8,128)S(1)} %get-tuple-element.22), channel_id=1, source_target_pairs={{64,0},{128,64},{192,128},{256,192},{320,256},{384,320},{448,384},... | collective-permute-start | bytes 307208 | tf_op jit(solution)/shard_map/ppermute | solution.py:676
  9.0 4.6 %collective-permute-done.1.right = f32[25,8,128]{2,1,0:T(8,128)S(1)} collective-permute-done((f32[25,8,128]{2,1,0:T(8,128)S(1)}, f32[25,8,128]{2,1,0:T(8,128)S(1)}, u32[]{:S(2)}, u32[]{:S(2)}) %collective-permute-start.1) | collective-permute-done | bytes 102432 | tf_op jit(solution)/shard_map/ppermute | solution.py:676
  13.7 3.5 %collective-permute-start.2 = (f32[520,128]{1,0:T(8,128)S(1)}, f32[520,128]{1,0:T(8,128)S(1)}, u32[]{:S(2)}, u32[]{:S(2)}) collective-permute-start(f32[520,128]{1,0:T(8,128)S(1)} %get-tuple-element.23), channel_id=1, source_target_pairs={{0,8},{8,16},{16,24},{24,32},{32,40},{40,48},{48,56},{1,9},{9,17},... | collective-permute-start | bytes 798728 | tf_op jit(solution)/shard_map/ppermute | solution.py:675
  17.2 2.4 %collective-permute-start.3 = (f32[520,128]{1,0:T(8,128)S(1)}, f32[520,128]{1,0:T(8,128)S(1)}, u32[]{:S(2)}, u32[]{:S(2)}) collective-permute-start(f32[520,128]{1,0:T(8,128)S(1)} %get-tuple-element.24), channel_id=1, source_target_pairs={{8,0},{16,8},{24,16},{32,24},{40,32},{48,40},{56,48},{9,1},{17,9},... | collective-permute-start | bytes 798728 | tf_op jit(solution)/shard_map/ppermute | solution.py:676
  19.6 3.0 %collective-permute-done.2.down = f32[520,128]{1,0:T(8,128)S(1)} collective-permute-done((f32[520,128]{1,0:T(8,128)S(1)}, f32[520,128]{1,0:T(8,128)S(1)}, u32[]{:S(2)}, u32[]{:S(2)}) %collective-permute-start.2) | collective-permute-done | bytes 266272 | tf_op jit(solution)/shard_map/ppermute | solution.py:675
  22.6 4.3 %collective-permute-done.3.up = f32[520,128]{1,0:T(8,128)S(1)} collective-permute-done((f32[520,128]{1,0:T(8,128)S(1)}, f32[520,128]{1,0:T(8,128)S(1)}, u32[]{:S(2)}, u32[]{:S(2)}) %collective-permute-start.3) | collective-permute-done | bytes 266272 | tf_op jit(solution)/shard_map/ppermute | solution.py:676
  26.9 1.1 %shard_map.43 = (f32[4,24,24,128]{3,2,1,0:T(8,128)S(1)}, f32[12,24,128]{2,1,0:T(8,128)S(1)}, f32[12,24,128]{2,1,0:T(8,128)S(1)}) custom-call(f32[4,8,8,128]{3,2,1,0:T(8,128)S(1)} %get-tuple-element.20.own, f32[25,8,128]{2,1,0:T(8,128)S(1)} %collective-permute-done.left, f32[25,8,128]{2,1,0:T(8,128)S(1)} %collective-permute-done.1.right, ...), custom_call_target="tpu_custom_call" | custom-call | tf_op jit(solution)/shard_map/pallas_call | solution.py:727
  28.0 1.9 %collective-permute-start.4 = (f32[12,24,128]{2,1,0:T(8,128)S(1)}, f32[12,24,128]{2,1,0:T(8,128)S(1)}, u32[]{:S(2)}, u32[]{:S(2)}) collective-permute-start(f32[12,24,128]{2,1,0:T(8,128)S(1)} %get-tuple-element.26), channel_id=1, source_target_pairs={{0,1},{1,2},{2,3},{3,4},{4,5},{5,6},{6,7},{8,9},{9,10},{10,11},{11... | collective-permute-start | bytes 442376 | tf_op jit(solution)/shard_map/ppermute | solution.py:675
  29.9 3.6 %collective-permute-start.5 = (f32[12,24,128]{2,1,0:T(8,128)S(1)}, f32[12,24,128]{2,1,0:T(8,128)S(1)}, u32[]{:S(2)}, u32[]{:S(2)}) collective-permute-start(f32[12,24,128]{2,1,0:T(8,128)S(1)} %get-tuple-element.27), channel_id=1, source_target_pairs={{1,0},{2,1},{3,2},{4,3},{5,4},{6,5},{7,6},{9,8},{10,9},{11,10},{12... | collective-permute-start | bytes 442376 | tf_op jit(solution)/shard_map/ppermute | solution.py:676
  33.5 0.9 %collective-permute-done.4.before = f32[12,24,128]{2,1,0:T(8,128)S(1)} collective-permute-done((f32[12,24,128]{2,1,0:T(8,128)S(1)}, f32[12,24,128]{2,1,0:T(8,128)S(1)}, u32[]{:S(2)}, u32[]{:S(2)}) %collective-permute-start.4) | collective-permute-done | bytes 147488 | tf_op jit(solution)/shard_map/ppermute | solution.py:675
  34.4 1.8 %collective-permute-done.5.after = f32[12,24,128]{2,1,0:T(8,128)S(1)} collective-permute-done((f32[12,24,128]{2,1,0:T(8,128)S(1)}, f32[12,24,128]{2,1,0:T(8,128)S(1)}, u32[]{:S(2)}, u32[]{:S(2)}) %collective-permute-start.5) | collective-permute-done | bytes 147488 | tf_op jit(solution)/shard_map/ppermute | solution.py:676
  36.2 11.9 %shard_map.44 = (f32[3,8,8,128]{3,2,1,0:T(8,128)S(1)}, f32[4,8,8,128]{3,2,1,0:T(8,128)S(1)}, f32[192,128]{1,0:T(8,128)S(1)}, f32[192,128]{1,0:T(8,128)S(1)}, f32...) custom-call(f32[4,24,24,128]{3,2,1,0:T(8,128)S(1)} %get-tuple-elemen, ...), custom_call_target="tpu_custom_call" | custom-call | tf_op jit(solution)/shard_map/pallas_call | solution.py:729
  48.1 5.5 %collective-permute-start.6 = (f32[192,128]{1,0:T(8,128)S(1)}, f32[192,128]{1,0:T(8,128)S(1)}, u32[]{:S(2)}, u32[]{:S(2)}) collective-permute-start(f32[192,128]{1,0:T(8,128)S(1)} %get-tuple-element.29), channel_id=1, source_target_pairs={{0,64},{64,128},{128,192},{192,256},{256,320},{320,384},{384,448},... | collective-permute-start | bytes 294920 | tf_op jit(solution)/shard_map/ppermute | solution.py:675
  53.6 1.9 %collective-permute-start.7 = (f32[192,128]{1,0:T(8,128)S(1)}, f32[192,128]{1,0:T(8,128)S(1)}, u32[]{:S(2)}, u32[]{:S(2)}) collective-permute-start(f32[192,128]{1,0:T(8,128)S(1)} %get-tuple-element.30), channel_id=1, source_target_pairs={{64,0},{128,64},{192,128},{256,192},{320,256},{384,320},{448,384},... | collective-permute-start | bytes 294920 | tf_op jit(solution)/shard_map/ppermute | solution.py:676
  55.5 0.8 collective-permute-done.6.left
  56.3 5.3 %collective-permute-done.7.right = f32[192,128]{1,0:T(8,128)S(1)} collective-permute-done((f32[192,128]{1,0:T(8,128)S(1)}, f32[192,128]{1,0:T(8,128)S(1)}, u32[]{:S(2)}, u32[]{:S(2)}) %collective-permute-start.7) | collective-permute-done | bytes 98336 | tf_op jit(solution)/shard_map/ppermute | solution.py:676
  61.7 4.9 %collective-permute-start.8 = (f32[368,128]{1,0:T(8,128)S(1)}, f32[368,128]{1,0:T(8,128)S(1)}, u32[]{:S(2)}, u32[]{:S(2)}) collective-permute-start(f32[368,128]{1,0:T(8,128)S(1)} %get-tuple-element.33), channel_id=1, source_target_pairs={{0,8},{8,16},{16,24},{24,32},{32,40},{40,48},{48,56},{1,9},{9,17},... | collective-permute-start | bytes 565256 | tf_op jit(solution)/shard_map/ppermute | solution.py:675
  66.6 1.9 %collective-permute-start.9 = (f32[368,128]{1,0:T(8,128)S(1)}, f32[368,128]{1,0:T(8,128)S(1)}, u32[]{:S(2)}, u32[]{:S(2)}) collective-permute-start(f32[368,128]{1,0:T(8,128)S(1)} %get-tuple-element.34), channel_id=1, source_target_pairs={{8,0},{16,8},{24,16},{32,24},{40,32},{48,40},{56,48},{9,1},{17,9},... | collective-permute-start | bytes 565256 | tf_op jit(solution)/shard_map/ppermute | solution.py:676
  68.5 2.4 %collective-permute-done.8.down = f32[368,128]{1,0:T(8,128)S(1)} collective-permute-done((f32[368,128]{1,0:T(8,128)S(1)}, f32[368,128]{1,0:T(8,128)S(1)}, u32[]{:S(2)}, u32[]{:S(2)}) %collective-permute-start.8) | collective-permute-done | bytes 188448 | tf_op jit(solution)/shard_map/ppermute | solution.py:675
  71.0 4.1 %collective-permute-done.9.up = f32[368,128]{1,0:T(8,128)S(1)} collective-permute-done((f32[368,128]{1,0:T(8,128)S(1)}, f32[368,128]{1,0:T(8,128)S(1)}, u32[]{:S(2)}, u32[]{:S(2)}) %collective-permute-start.9) | collective-permute-done | bytes 188448 | tf_op jit(solution)/shard_map/ppermute | solution.py:676
  75.1 10.6 %shard_map.46 = (f32[3,8,8,128]{3,2,1,0:T(8,128)}, f32[3,4,4,64]{3,2,1,0:T(4,128)}) custom-call(f32[4,8,8,128]{3,2,1,0:T(8,128)S(1)} %get-tuple-element.28.own, f32[192,128]{1,0:T(8,128)S(1)} %collective-permute-done.6.left, f32[192,128]{1,0:T(8,128)S(1)} %collective-permute-done.7.right, f32[368,128]{1,0:T(8,128)S(1)} %collective-permute-done.8.down, ...), custom_call_target="tpu_custom_call" | custom-call | tf_op jit(solution)/shard_map/pallas_call | solution.py:735
  (6 shorter events, 0.6 us)
Async XLA Ops:
  0.6 0.9 %copy-start = (f32[3,8,8,128]{3,2,1,0:T(8,128)S(1)}, f32[3,8,8,128]{3,2,1,0:T(8,128)}, u32[]{:S(2)}) copy-start(f32[3,8,8,128]{3,2,1,0:T(8,128)} %residual.1) | copy-start | bytes 294916
  1.5 0.8 copy-start.1
  2.5 6.6 %collective-permute-start = (f32[25,8,128]{2,1,0:T(8,128)S(1)}, f32[25,8,128]{2,1,0:T(8,128)S(1)}, u32[]{:S(2)}, u32[]{:S(2)}) collective-permute-start(f32[25,8,128]{2,1,0:T(8,128)S(1)} %get-tuple-element.21), channel_id=1, source_target_pairs={{0,64},{64,128},{128,192},{192,256},{256,320},{320,384},{384,448},... | collective-permute-start | bytes 307208 | tf_op jit(solution)/shard_map/ppermute | solution.py:675
  6.8 6.9 %collective-permute-start.1 = (f32[25,8,128]{2,1,0:T(8,128)S(1)}, f32[25,8,128]{2,1,0:T(8,128)S(1)}, u32[]{:S(2)}, u32[]{:S(2)}) collective-permute-start(f32[25,8,128]{2,1,0:T(8,128)S(1)} %get-tuple-element.22), channel_id=1, source_target_pairs={{64,0},{128,64},{192,128},{256,192},{320,256},{384,320},{448,384},... | collective-permute-start | bytes 307208 | tf_op jit(solution)/shard_map/ppermute | solution.py:676
  13.7 8.9 %collective-permute-start.2 = (f32[520,128]{1,0:T(8,128)S(1)}, f32[520,128]{1,0:T(8,128)S(1)}, u32[]{:S(2)}, u32[]{:S(2)}) collective-permute-start(f32[520,128]{1,0:T(8,128)S(1)} %get-tuple-element.23), channel_id=1, source_target_pairs={{0,8},{8,16},{16,24},{24,32},{32,40},{40,48},{48,56},{1,9},{9,17},... | collective-permute-start | bytes 798728 | tf_op jit(solution)/shard_map/ppermute | solution.py:675
  17.2 9.7 %collective-permute-start.3 = (f32[520,128]{1,0:T(8,128)S(1)}, f32[520,128]{1,0:T(8,128)S(1)}, u32[]{:S(2)}, u32[]{:S(2)}) collective-permute-start(f32[520,128]{1,0:T(8,128)S(1)} %get-tuple-element.24), channel_id=1, source_target_pairs={{8,0},{16,8},{24,16},{32,24},{40,32},{48,40},{56,48},{9,1},{17,9},... | collective-permute-start | bytes 798728 | tf_op jit(solution)/shard_map/ppermute | solution.py:676
  28.0 6.5 %collective-permute-start.4 = (f32[12,24,128]{2,1,0:T(8,128)S(1)}, f32[12,24,128]{2,1,0:T(8,128)S(1)}, u32[]{:S(2)}, u32[]{:S(2)}) collective-permute-start(f32[12,24,128]{2,1,0:T(8,128)S(1)} %get-tuple-element.26), channel_id=1, source_target_pairs={{0,1},{1,2},{2,3},{3,4},{4,5},{5,6},{6,7},{8,9},{9,10},{10,11},{11... | collective-permute-start | bytes 442376 | tf_op jit(solution)/shard_map/ppermute | solution.py:675
  29.9 6.3 %collective-permute-start.5 = (f32[12,24,128]{2,1,0:T(8,128)S(1)}, f32[12,24,128]{2,1,0:T(8,128)S(1)}, u32[]{:S(2)}, u32[]{:S(2)}) collective-permute-start(f32[12,24,128]{2,1,0:T(8,128)S(1)} %get-tuple-element.27), channel_id=1, source_target_pairs={{1,0},{2,1},{3,2},{4,3},{5,4},{6,5},{7,6},{9,8},{10,9},{11,10},{12... | collective-permute-start | bytes 442376 | tf_op jit(solution)/shard_map/ppermute | solution.py:676
  48.1 8.2 %collective-permute-start.6 = (f32[192,128]{1,0:T(8,128)S(1)}, f32[192,128]{1,0:T(8,128)S(1)}, u32[]{:S(2)}, u32[]{:S(2)}) collective-permute-start(f32[192,128]{1,0:T(8,128)S(1)} %get-tuple-element.29), channel_id=1, source_target_pairs={{0,64},{64,128},{128,192},{192,256},{256,320},{320,384},{384,448},... | collective-permute-start | bytes 294920 | tf_op jit(solution)/shard_map/ppermute | solution.py:675
  53.6 8.1 %collective-permute-start.7 = (f32[192,128]{1,0:T(8,128)S(1)}, f32[192,128]{1,0:T(8,128)S(1)}, u32[]{:S(2)}, u32[]{:S(2)}) collective-permute-start(f32[192,128]{1,0:T(8,128)S(1)} %get-tuple-element.30), channel_id=1, source_target_pairs={{64,0},{128,64},{192,128},{256,192},{320,256},{384,320},{448,384},... | collective-permute-start | bytes 294920 | tf_op jit(solution)/shard_map/ppermute | solution.py:676
  61.7 9.2 %collective-permute-start.8 = (f32[368,128]{1,0:T(8,128)S(1)}, f32[368,128]{1,0:T(8,128)S(1)}, u32[]{:S(2)}, u32[]{:S(2)}) collective-permute-start(f32[368,128]{1,0:T(8,128)S(1)} %get-tuple-element.33), channel_id=1, source_target_pairs={{0,8},{8,16},{16,24},{24,32},{32,40},{40,48},{48,56},{1,9},{9,17},... | collective-permute-start | bytes 565256 | tf_op jit(solution)/shard_map/ppermute | solution.py:675
  66.6 8.5 %collective-permute-start.9 = (f32[368,128]{1,0:T(8,128)S(1)}, f32[368,128]{1,0:T(8,128)S(1)}, u32[]{:S(2)}, u32[]{:S(2)}) collective-permute-start(f32[368,128]{1,0:T(8,128)S(1)} %get-tuple-element.34), channel_id=1, source_target_pairs={{8,0},{16,8},{24,16},{32,24},{40,32},{48,40},{56,48},{9,1},{17,9},... | collective-permute-start | bytes 565256 | tf_op jit(solution)/shard_map/ppermute | solution.py:676
where the time goes:
time: 86.1 us; the launch traced here: 85.7 us
  starting transfers between devices  31.8 us (37%)
  waiting for transfers between devices  27.6 us (32%)
  Pallas kernels  23.9 us (28%)
  local copies, waits for them, and re-layouts  1.64 us (2%)
    ppermute x5, waiting for transfers between devices, neighbours(): lax.ppermute(to_previous, axis, [(i + 1, i) for i in range(count - 1)])  20.1 us
    ppermute x5, starting transfers between devices, neighbours(): before = lax.ppermute(to_next, axis, [(i, i + 1) for i in range(count - 1)])  20 us
    pallas_call x1, Pallas kernels, on_device(): call(smooth_kernel, SMOOTH_OUTS, SMOOTH_SCRATCH)(main, before, after)  11.9 us
    ppermute x5, starting transfers between devices, neighbours(): lax.ppermute(to_previous, axis, [(i + 1, i) for i in range(count - 1)])  11.8 us
    pallas_call x1, Pallas kernels, on_device(): call(post_kernel, POST_OUTS, POST_SCRATCH)  10.6 us
    ppermute x5, waiting for transfers between devices, neighbours(): before = lax.ppermute(to_next, axis, [(i, i + 1) for i in range(count - 1)])  7.49 us
  transfers between devices with their start and end apart: 10, of which 10 were waited for; matrix products, arithmetic and copies ran while one was open for 0% of the time, Pallas kernels for 0%

commit v1 on v0

--- a/solution.py
+++ b/solution.py
@@ -14,7 +14,6 @@
 WHOLE = 1.92
 HALO = 16
 CHUNKS = (4, 3, 2, 1)
-FAR = pltpu.HBM
 
 
 def sweep_scales():
@@ -138,7 +137,7 @@
     lane, begins = side_lanes()
     inward = pltpu.roll(side, 112, 1)
     side_below, side_above = side, side
-    for g in range(4):
+    for g in range(3):
         outward = pltpu.roll(main, 32 * g + HALO, 1)
         side_above = jnp.where(lane == 32 * g + HALO, outward, side_above)
         side_below = jnp.where(lane == 32 * g + HALO - 1, outward, side_below)
@@ -245,31 +244,17 @@
     return jnp.dot(a, b, precision=lax.Precision.HIGHEST, preferred_element_type=jnp.float32)
 
 
-def prepare(levels, residual, own, ahead, behind, held_levels, held_residual, sems):
-    copies = [
-        pltpu.make_async_copy(levels, held_levels, sems.at[0]),
-        pltpu.make_async_copy(residual, held_residual, sems.at[1]),
-    ]
-    for copy in copies:
-        copy.start()
-    copies[0].wait()
+def pack_planes(own, ahead, behind):
     for p in range(8):
-        ratio = held_levels[p].astype(jnp.float32) / 255.0
-        value = (0.05 + 0.95 * ratio * ratio * ratio) / UNIT
-        own[3, p] = value
         if p > 0:
-            ahead[p - 1] = value
+            ahead[p - 1] = own[3, p]
         if p < 7:
-            behind[p] = value
-    copies[1].wait()
-    for c in range(3):
-        for p in range(8):
-            value = held_residual[c, p]
-            own[c, p] = value
+            behind[p] = own[3, p]
+        for c in range(3):
             if p > 1:
-                ahead[7 + 6 * c + p - 2] = value
+                ahead[7 + 6 * c + p - 2] = own[c, p]
             if p < 6:
-                behind[7 + 6 * c + p] = value
+                behind[7 + 6 * c + p] = own[c, p]
 
 
 def fine_planes(own, left, right):
@@ -299,7 +284,7 @@
     return (7 * (plane - 1), 7) if c == 3 else (154 + 6 * (20 * c + plane - 2), 6)
 
 
-def pack_rows(own, left, right, ahead, behind):
+def pack_rows(own, right, left, ahead, behind):
     empty = jnp.zeros((8, 128), jnp.float32)
     ahead[pl.ds(FINE_ROWS - 8, 8), :] = empty
     behind[pl.ds(FINE_ROWS - 8, 8), :] = empty
@@ -309,7 +294,7 @@
         behind[pl.ds(base, count), :] = source[(*index, pl.ds(0, count), slice(None))]
 
 
-def pack_lanes(own, left, right, down, up, main, first, last):
+def pack_lanes(own, right, left, up, down, main, first, last):
     empty = jnp.zeros((24, 128), jnp.float32)
     for plane in (0, 1, 22, 23):
         for c in range(3):
@@ -374,7 +359,7 @@
     return (6 * plane, 6, 2) if c == 3 else (96 + 5 * (14 * c + plane - 1), 5, 1)
 
 
-def pack_coarse(own, left, right, layer_ahead, layer_behind, ahead, behind):
+def pack_coarse(own, right, left, layer_ahead, layer_behind, ahead, behind):
     empty = jnp.zeros((8, 128), jnp.float32)
     for message, layer, offset in ((ahead, layer_ahead, 7), (behind, layer_behind, 4)):
         message[pl.ds(COARSE_ROWS_Y - 8, 8), :] = empty
@@ -390,7 +375,7 @@
 
 
 def smooth_kernel(
-    main, before, after, smooth, message, ahead, behind, layer_ahead, layer_behind, state, side_state,
+    main, after, before, smooth, message, ahead, behind, layer_ahead, layer_behind, state, side_state,
     ua, ub, va, vb, usa, usb, vsa, vsb, rest, modulus, diag, inverse, prev, next, rest_s, modulus_s, diag_s, inverse_s, prev_s, next_s, pairs, pairs_s,
 ):
     group = lane_index() // 32
@@ -524,7 +509,7 @@
 
 
 def post_kernel(
-    own, left, right, down, up, state_in, side_in, smooth, correction, coarse,
+    own, right, left, up, down, state_in, side_in, smooth, correction, coarse,
     ca, cb, cva, cvb, crest, cmod, cinv, cdiag, cprev, cnext, total, ua, ub, va, vb, usa, usb, vsa, vsb, wide, wide_s, rest, rest_s,
 ):
     scales = sweep_scales()
@@ -584,7 +569,7 @@
     coarse_moduli = [[reader(cmod, 8), reader(cprev, 0), reader(cnext, 0)]]
     for k in range(1, SWEEPS):
         now, later = ((ca, cva), (cb, cvb)) if k % 2 else ((cb, cvb), (ca, cva))
-        sweep((1 + k, 15 - k), (0, 8), now, later, (crest,), coarse_moduli, [reader(cdiag, 0)], [reader(cinv, 0)], scales[k - 1])
+        sweep((1 + k, 15 - k), (0, 8) if k < 3 else (4,), now, later, (crest,), coarse_moduli, [reader(cdiag, 0)], [reader(cinv, 0)], scales[k - 1])
         gather(later[0], False)
 
     for c in range(3):
@@ -660,20 +645,19 @@
             add_own(later[0], False)
 
 
-def call(kernel, outs, scratch=(), far=False, extra=()):
+def call(kernel, outs, scratch=()):
     return pl.pallas_call(
         kernel,
         out_shape=[jax.ShapeDtypeStruct(s, jnp.float32) for s in outs],
-        **(dict(in_specs=[pl.BlockSpec(memory_space=FAR)] * 2) if far else {}),
-        scratch_shapes=[pltpu.VMEM(s, jnp.float32) for s in scratch] + list(extra),
+        scratch_shapes=[pltpu.VMEM(s, jnp.float32) for s in scratch],
         compiler_params=pltpu.CompilerParams(vmem_limit_bytes=48 * 1024 * 1024),
     )
 
 
 def neighbours(to_next, to_previous, axis):
     count = lax.axis_size(axis)
+    after = lax.ppermute(to_previous, axis, [(i + 1, i) for i in range(count - 1)])
     before = lax.ppermute(to_next, axis, [(i, i + 1) for i in range(count - 1)])
-    after = lax.ppermute(to_previous, axis, [(i + 1, i) for i in range(count - 1)])
     return before, after
 
 
@@ -715,24 +699,22 @@
 
 
 def on_device(levels, residual):
-    own, ahead, behind = call(
-        prepare,
-        [(4, 8, 8, 128), (25, 8, 128), (25, 8, 128)],
-        far=True,
-        extra=[pltpu.VMEM((8, 8, 128), jnp.int32), pltpu.VMEM((3, 8, 8, 128), jnp.float32), pltpu.SemaphoreType.DMA((2,))],
-    )(levels, residual)
+    ratio = levels.astype(jnp.float32) / 255.0
+    modulus = (0.05 + 0.95 * ratio * ratio * ratio) / UNIT
+    own = jnp.concatenate([residual, modulus[None]])
+    ahead, behind = call(pack_planes, [(25, 8, 128), (25, 8, 128)])(own)
     left, right = neighbours(ahead, behind, "gx")
-    ahead, behind = call(pack_rows, [(FINE_ROWS, 128)] * 2)(own, left, right)
+    ahead, behind = call(pack_rows, [(FINE_ROWS, 128)] * 2)(own, right, left)
     down, up = neighbours(ahead, behind, "gy")
-    main, first, last = call(pack_lanes, [(4, 24, 24, 128), (12, 24, 128), (12, 24, 128)])(own, left, right, down, up)
+    main, first, last = call(pack_lanes, [(4, 24, 24, 128), (12, 24, 128), (12, 24, 128)])(own, right, left, up, down)
     before, after = neighbours(last, first, "gz")
     smooth, own, ahead, behind, layer_ahead, layer_behind, state, side_state = call(
         smooth_kernel, SMOOTH_OUTS, SMOOTH_SCRATCH
-    )(main, before, after)
+    )(main, after, before)
     left, right = neighbours(ahead, behind, "gx")
-    ahead, behind = call(pack_coarse, [(COARSE_ROWS_Y, 128)] * 2)(own, left, right, layer_ahead, layer_behind)
+    ahead, behind = call(pack_coarse, [(COARSE_ROWS_Y, 128)] * 2)(own, right, left, layer_ahead, layer_behind)
     down, up = neighbours(ahead, behind, "gy")
-    correction, coarse = call(post_kernel, POST_OUTS, POST_SCRATCH)(own, left, right, down, up, state, side_state, smooth)
+    correction, coarse = call(post_kernel, POST_OUTS, POST_SCRATCH)(own, right, left, up, down, state, side_state, smooth)
     return correction, coarse
 
 

time: 86.1 us -> 76.9 us (0.89)
  the two profiles are of different devices: /device:TPU:84 before, /device:TPU:302 now
where the time goes in v1:
time: 76.9 us; the launch traced here: 76.5 us
  starting transfers between devices  27.7 us (36%)
  Pallas kernels  23.5 us (31%)
  waiting for transfers between devices  22.9 us (30%)
  other arithmetic  1.68 us (2%)
    ppermute x5, waiting for transfers between devices, neighbours(): before = lax.ppermute(to_next, axis, [(i, i + 1) for i in range(count - 1)])  16.6 us
    ppermute x5, starting transfers between devices, neighbours(): before = lax.ppermute(to_next, axis, [(i, i + 1) for i in range(count - 1)])  15.1 us
    ppermute x5, starting transfers between devices, neighbours(): lax.ppermute(to_previous, axis, [(i + 1, i) for i in range(count - 1)])  12.6 us
    pallas_call x1, Pallas kernels, on_device(): call(smooth_kernel, SMOOTH_OUTS, SMOOTH_SCRATCH)(main, after, before)  11.9 us
    pallas_call x1, Pallas kernels, on_device(): call(post_kernel, POST_OUTS, POST_SCRATCH)  10.4 us
    ppermute x5, waiting for transfers between devices, neighbours(): lax.ppermute(to_previous, axis, [(i + 1, i) for i in range(count - 1)])  6.22 us
  transfers between devices with their start and end apart: 10, of which 10 were waited for; matrix products, arithmetic and copies ran while one was open for 0% of the time, Pallas kernels for 0%

profile of v1, /device:TPU:302, one launch (start us, length us, event | category | flops | bytes accessed | tf_op | source)
XLA Modules:
  0.0 76.5 jit_solution(509445582389843006)
XLA Ops:
  0.6 0.8 %fusion.2 = f32[1,8,8,128]{3,2,1,0:T(8,128)S(1)} fusion(s32[8,8,128]{2,1,0:T(8,128)} %param.2), kind=kLoop, calls=%fused_computation.4 | loop fusion | flops 57344 | bytes 65536 | tf_op jit(solution)/shard_map/broadcast_in_dim | solution.py:704
  1.4 0.9 %pad_maximum_fusion.own = f32[4,8,8,128]{3,2,1,0:T(8,128)S(1)} fusion(f32[1,8,8,128]{3,2,1,0:T(8,128)S(1)} %fusion.2, f32[3,8,8,128]{3,2,1,0:T(8,128)} %param.3), kind=kLoop, calls=%fused_computation | loop fusion | flops 32768 | bytes 262144 | tf_op jit(solution)/shard_map/concatenate | solution.py:704
  2.3 1.9 %collective-permute-start = (f32[25,8,128]{2,1,0:T(8,128)S(1)}, f32[25,8,128]{2,1,0:T(8,128)S(1)}, u32[]{:S(2)}, u32[]{:S(2)}) collective-permute-start(f32[25,8,128]{2,1,0:T(8,128)S(1)} %get-tuple-element.19), channel_id=1, source_target_pairs={{64,0},{128,64},{192,128},{256,192},{320,256},{384,320},{448,384},... | collective-permute-start | bytes 307208 | tf_op jit(solution)/shard_map/ppermute | solution.py:659
  4.3 3.9 %collective-permute-start.1 = (f32[25,8,128]{2,1,0:T(8,128)S(1)}, f32[25,8,128]{2,1,0:T(8,128)S(1)}, u32[]{:S(2)}, u32[]{:S(2)}) collective-permute-start(f32[25,8,128]{2,1,0:T(8,128)S(1)} %get-tuple-element.20), channel_id=1, source_target_pairs={{0,64},{64,128},{128,192},{192,256},{256,320},{320,384},{384,448},... | collective-permute-start | bytes 307208 | tf_op jit(solution)/shard_map/ppermute | solution.py:660
  8.2 0.7 collective-permute-done.right
  8.9 3.1 %collective-permute-done.1.left = f32[25,8,128]{2,1,0:T(8,128)S(1)} collective-permute-done((f32[25,8,128]{2,1,0:T(8,128)S(1)}, f32[25,8,128]{2,1,0:T(8,128)S(1)}, u32[]{:S(2)}, u32[]{:S(2)}) %collective-permute-start.1) | collective-permute-done | bytes 102432 | tf_op jit(solution)/shard_map/ppermute | solution.py:660
  12.1 3.3 %collective-permute-start.2 = (f32[520,128]{1,0:T(8,128)S(1)}, f32[520,128]{1,0:T(8,128)S(1)}, u32[]{:S(2)}, u32[]{:S(2)}) collective-permute-start(f32[520,128]{1,0:T(8,128)S(1)} %get-tuple-element.21), channel_id=1, source_target_pairs={{8,0},{16,8},{24,16},{32,24},{40,32},{48,40},{56,48},{9,1},{17,9},... | collective-permute-start | bytes 798728 | tf_op jit(solution)/shard_map/ppermute | solution.py:659
  15.4 2.6 %collective-permute-start.3 = (f32[520,128]{1,0:T(8,128)S(1)}, f32[520,128]{1,0:T(8,128)S(1)}, u32[]{:S(2)}, u32[]{:S(2)}) collective-permute-start(f32[520,128]{1,0:T(8,128)S(1)} %get-tuple-element.22), channel_id=1, source_target_pairs={{0,8},{8,16},{16,24},{24,32},{32,40},{40,48},{48,56},{1,9},{9,17},... | collective-permute-start | bytes 798728 | tf_op jit(solution)/shard_map/ppermute | solution.py:660
  18.0 3.0 %collective-permute-done.2.up = f32[520,128]{1,0:T(8,128)S(1)} collective-permute-done((f32[520,128]{1,0:T(8,128)S(1)}, f32[520,128]{1,0:T(8,128)S(1)}, u32[]{:S(2)}, u32[]{:S(2)}) %collective-permute-start.2) | collective-permute-done | bytes 266272 | tf_op jit(solution)/shard_map/ppermute | solution.py:659
  21.0 3.0 %collective-permute-done.3.down = f32[520,128]{1,0:T(8,128)S(1)} collective-permute-done((f32[520,128]{1,0:T(8,128)S(1)}, f32[520,128]{1,0:T(8,128)S(1)}, u32[]{:S(2)}, u32[]{:S(2)}) %collective-permute-start.3) | collective-permute-done | bytes 266272 | tf_op jit(solution)/shard_map/ppermute | solution.py:660
  24.0 1.1 %shard_map.43 = (f32[4,24,24,128]{3,2,1,0:T(8,128)S(1)}, f32[12,24,128]{2,1,0:T(8,128)S(1)}, f32[12,24,128]{2,1,0:T(8,128)S(1)}) custom-call(f32[4,8,8,128]{3,2,1,0:T(8,128)S(1)} %pad_maximum_fusion.own, f32[25,8,128]{2,1,0:T(8,128)S(1)} %collective-permute-done.right, f32[25,8,128]{2,1,0:T(8,128)S(1)} %collective-permute-done.1.left, ...), custom_call_target="tpu_custom_call" | custom-call | tf_op jit(solution)/shard_map/pallas_call | solution.py:709
  25.0 1.9 %collective-permute-start.4 = (f32[12,24,128]{2,1,0:T(8,128)S(1)}, f32[12,24,128]{2,1,0:T(8,128)S(1)}, u32[]{:S(2)}, u32[]{:S(2)}) collective-permute-start(f32[12,24,128]{2,1,0:T(8,128)S(1)} %get-tuple-element.24), channel_id=1, source_target_pairs={{1,0},{2,1},{3,2},{4,3},{5,4},{6,5},{7,6},{9,8},{10,9},{11,10},{12... | collective-permute-start | bytes 442376 | tf_op jit(solution)/shard_map/ppermute | solution.py:659
  27.0 2.4 %collective-permute-start.5 = (f32[12,24,128]{2,1,0:T(8,128)S(1)}, f32[12,24,128]{2,1,0:T(8,128)S(1)}, u32[]{:S(2)}, u32[]{:S(2)}) collective-permute-start(f32[12,24,128]{2,1,0:T(8,128)S(1)} %get-tuple-element.25), channel_id=1, source_target_pairs={{0,1},{1,2},{2,3},{3,4},{4,5},{5,6},{6,7},{8,9},{9,10},{10,11},{11... | collective-permute-start | bytes 442376 | tf_op jit(solution)/shard_map/ppermute | solution.py:660
  29.6 3.8 %collective-permute-done.5.before = f32[12,24,128]{2,1,0:T(8,128)S(1)} collective-permute-done((f32[12,24,128]{2,1,0:T(8,128)S(1)}, f32[12,24,128]{2,1,0:T(8,128)S(1)}, u32[]{:S(2)}, u32[]{:S(2)}) %collective-permute-start.5) | collective-permute-done | bytes 147488 | tf_op jit(solution)/shard_map/ppermute | solution.py:660
  33.4 11.9 %shard_map.44 = (f32[3,8,8,128]{3,2,1,0:T(8,128)S(1)}, f32[4,8,8,128]{3,2,1,0:T(8,128)S(1)}, f32[192,128]{1,0:T(8,128)S(1)}, f32[192,128]{1,0:T(8,128)S(1)}, f32...) custom-call(f32[4,24,24,128]{3,2,1,0:T(8,128)S(1)} %get-tuple-elemen, ...), custom_call_target="tpu_custom_call" | custom-call | tf_op jit(solution)/shard_map/pallas_call | solution.py:711
  45.3 1.9 %collective-permute-start.6 = (f32[192,128]{1,0:T(8,128)S(1)}, f32[192,128]{1,0:T(8,128)S(1)}, u32[]{:S(2)}, u32[]{:S(2)}) collective-permute-start(f32[192,128]{1,0:T(8,128)S(1)} %get-tuple-element.27), channel_id=1, source_target_pairs={{64,0},{128,64},{192,128},{256,192},{320,256},{384,320},{448,384},... | collective-permute-start | bytes 294920 | tf_op jit(solution)/shard_map/ppermute | solution.py:659
  47.2 3.9 %collective-permute-start.7 = (f32[192,128]{1,0:T(8,128)S(1)}, f32[192,128]{1,0:T(8,128)S(1)}, u32[]{:S(2)}, u32[]{:S(2)}) collective-permute-start(f32[192,128]{1,0:T(8,128)S(1)} %get-tuple-element.28), channel_id=1, source_target_pairs={{0,64},{64,128},{128,192},{192,256},{256,320},{320,384},{384,448},... | collective-permute-start | bytes 294920 | tf_op jit(solution)/shard_map/ppermute | solution.py:660
  51.2 0.7 collective-permute-done.6.right
  51.8 3.1 %collective-permute-done.7.left = f32[192,128]{1,0:T(8,128)S(1)} collective-permute-done((f32[192,128]{1,0:T(8,128)S(1)}, f32[192,128]{1,0:T(8,128)S(1)}, u32[]{:S(2)}, u32[]{:S(2)}) %collective-permute-start.7) | collective-permute-done | bytes 98336 | tf_op jit(solution)/shard_map/ppermute | solution.py:660
  55.0 3.6 %collective-permute-start.8 = (f32[368,128]{1,0:T(8,128)S(1)}, f32[368,128]{1,0:T(8,128)S(1)}, u32[]{:S(2)}, u32[]{:S(2)}) collective-permute-start(f32[368,128]{1,0:T(8,128)S(1)} %get-tuple-element.31), channel_id=1, source_target_pairs={{8,0},{16,8},{24,16},{32,24},{40,32},{48,40},{56,48},{9,1},{17,9},... | collective-permute-start | bytes 565256 | tf_op jit(solution)/shard_map/ppermute | solution.py:659
  58.6 2.3 %collective-permute-start.9 = (f32[368,128]{1,0:T(8,128)S(1)}, f32[368,128]{1,0:T(8,128)S(1)}, u32[]{:S(2)}, u32[]{:S(2)}) collective-permute-start(f32[368,128]{1,0:T(8,128)S(1)} %get-tuple-element.32), channel_id=1, source_target_pairs={{0,8},{8,16},{16,24},{24,32},{32,40},{40,48},{48,56},{1,9},{9,17},... | collective-permute-start | bytes 565256 | tf_op jit(solution)/shard_map/ppermute | solution.py:660
  60.9 1.6 %collective-permute-done.8.up = f32[368,128]{1,0:T(8,128)S(1)} collective-permute-done((f32[368,128]{1,0:T(8,128)S(1)}, f32[368,128]{1,0:T(8,128)S(1)}, u32[]{:S(2)}, u32[]{:S(2)}) %collective-permute-start.8) | collective-permute-done | bytes 188448 | tf_op jit(solution)/shard_map/ppermute | solution.py:659
  62.5 3.6 %collective-permute-done.9.down = f32[368,128]{1,0:T(8,128)S(1)} collective-permute-done((f32[368,128]{1,0:T(8,128)S(1)}, f32[368,128]{1,0:T(8,128)S(1)}, u32[]{:S(2)}, u32[]{:S(2)}) %collective-permute-start.9) | collective-permute-done | bytes 188448 | tf_op jit(solution)/shard_map/ppermute | solution.py:660
  66.1 10.4 %shard_map.46 = (f32[3,8,8,128]{3,2,1,0:T(8,128)}, f32[3,4,4,64]{3,2,1,0:T(4,128)}) custom-call(f32[4,8,8,128]{3,2,1,0:T(8,128)S(1)} %get-tuple-element.26.own, f32[192,128]{1,0:T(8,128)S(1)} %collective-permute-done.6.right, f32[192,128]{1,0:T(8,128)S(1)} %collective-permute-done.7.left, f32[368,128]{1,0:T(8,128)S(1)} %collective-permute-done.8.up, ...), custom_call_target="tpu_custom_call" | custom-call | tf_op jit(solution)/shard_map/pallas_call | solution.py:717
  (4 shorter events, 0.4 us)
Async XLA Ops:
  2.3 6.6 %collective-permute-start = (f32[25,8,128]{2,1,0:T(8,128)S(1)}, f32[25,8,128]{2,1,0:T(8,128)S(1)}, u32[]{:S(2)}, u32[]{:S(2)}) collective-permute-start(f32[25,8,128]{2,1,0:T(8,128)S(1)} %get-tuple-element.19), channel_id=1, source_target_pairs={{64,0},{128,64},{192,128},{256,192},{320,256},{384,320},{448,384},... | collective-permute-start | bytes 307208 | tf_op jit(solution)/shard_map/ppermute | solution.py:659
  4.3 7.8 %collective-permute-start.1 = (f32[25,8,128]{2,1,0:T(8,128)S(1)}, f32[25,8,128]{2,1,0:T(8,128)S(1)}, u32[]{:S(2)}, u32[]{:S(2)}) collective-permute-start(f32[25,8,128]{2,1,0:T(8,128)S(1)} %get-tuple-element.20), channel_id=1, source_target_pairs={{0,64},{64,128},{128,192},{192,256},{256,320},{320,384},{384,448},... | collective-permute-start | bytes 307208 | tf_op jit(solution)/shard_map/ppermute | solution.py:660
  12.1 8.9 %collective-permute-start.2 = (f32[520,128]{1,0:T(8,128)S(1)}, f32[520,128]{1,0:T(8,128)S(1)}, u32[]{:S(2)}, u32[]{:S(2)}) collective-permute-start(f32[520,128]{1,0:T(8,128)S(1)} %get-tuple-element.21), channel_id=1, source_target_pairs={{8,0},{16,8},{24,16},{32,24},{40,32},{48,40},{56,48},{9,1},{17,9},... | collective-permute-start | bytes 798728 | tf_op jit(solution)/shard_map/ppermute | solution.py:659
  15.4 8.6 %collective-permute-start.3 = (f32[520,128]{1,0:T(8,128)S(1)}, f32[520,128]{1,0:T(8,128)S(1)}, u32[]{:S(2)}, u32[]{:S(2)}) collective-permute-start(f32[520,128]{1,0:T(8,128)S(1)} %get-tuple-element.22), channel_id=1, source_target_pairs={{0,8},{8,16},{16,24},{24,32},{32,40},{40,48},{48,56},{1,9},{9,17},... | collective-permute-start | bytes 798728 | tf_op jit(solution)/shard_map/ppermute | solution.py:660
  25.0 4.6 %collective-permute-start.4 = (f32[12,24,128]{2,1,0:T(8,128)S(1)}, f32[12,24,128]{2,1,0:T(8,128)S(1)}, u32[]{:S(2)}, u32[]{:S(2)}) collective-permute-start(f32[12,24,128]{2,1,0:T(8,128)S(1)} %get-tuple-element.24), channel_id=1, source_target_pairs={{1,0},{2,1},{3,2},{4,3},{5,4},{6,5},{7,6},{9,8},{10,9},{11,10},{12... | collective-permute-start | bytes 442376 | tf_op jit(solution)/shard_map/ppermute | solution.py:659
  27.0 6.5 %collective-permute-start.5 = (f32[12,24,128]{2,1,0:T(8,128)S(1)}, f32[12,24,128]{2,1,0:T(8,128)S(1)}, u32[]{:S(2)}, u32[]{:S(2)}) collective-permute-start(f32[12,24,128]{2,1,0:T(8,128)S(1)} %get-tuple-element.25), channel_id=1, source_target_pairs={{0,1},{1,2},{2,3},{3,4},{4,5},{5,6},{6,7},{8,9},{9,10},{10,11},{11... | collective-permute-start | bytes 442376 | tf_op jit(solution)/shard_map/ppermute | solution.py:660
  45.3 6.5 %collective-permute-start.6 = (f32[192,128]{1,0:T(8,128)S(1)}, f32[192,128]{1,0:T(8,128)S(1)}, u32[]{:S(2)}, u32[]{:S(2)}) collective-permute-start(f32[192,128]{1,0:T(8,128)S(1)} %get-tuple-element.27), channel_id=1, source_target_pairs={{64,0},{128,64},{192,128},{256,192},{320,256},{384,320},{448,384},... | collective-permute-start | bytes 294920 | tf_op jit(solution)/shard_map/ppermute | solution.py:659
  47.2 7.7 %collective-permute-start.7 = (f32[192,128]{1,0:T(8,128)S(1)}, f32[192,128]{1,0:T(8,128)S(1)}, u32[]{:S(2)}, u32[]{:S(2)}) collective-permute-start(f32[192,128]{1,0:T(8,128)S(1)} %get-tuple-element.28), channel_id=1, source_target_pairs={{0,64},{64,128},{128,192},{192,256},{256,320},{320,384},{384,448},... | collective-permute-start | bytes 294920 | tf_op jit(solution)/shard_map/ppermute | solution.py:660
  55.0 7.5 %collective-permute-start.8 = (f32[368,128]{1,0:T(8,128)S(1)}, f32[368,128]{1,0:T(8,128)S(1)}, u32[]{:S(2)}, u32[]{:S(2)}) collective-permute-start(f32[368,128]{1,0:T(8,128)S(1)} %get-tuple-element.31), channel_id=1, source_target_pairs={{8,0},{16,8},{24,16},{32,24},{40,32},{48,40},{56,48},{9,1},{17,9},... | collective-permute-start | bytes 565256 | tf_op jit(solution)/shard_map/ppermute | solution.py:659
  58.6 7.5 %collective-permute-start.9 = (f32[368,128]{1,0:T(8,128)S(1)}, f32[368,128]{1,0:T(8,128)S(1)}, u32[]{:S(2)}, u32[]{:S(2)}) collective-permute-start(f32[368,128]{1,0:T(8,128)S(1)} %get-tuple-element.32), channel_id=1, source_target_pairs={{0,8},{8,16},{16,24},{24,32},{32,40},{40,48},{48,56},{1,9},{9,17},... | collective-permute-start | bytes 565256 | tf_op jit(solution)/shard_map/ppermute | solution.py:660

commit v2 on v1

--- a/solution.py
+++ b/solution.py
@@ -13,7 +13,8 @@
 UNIT = 120.0
 WHOLE = 1.92
 HALO = 16
-CHUNKS = (4, 3, 2, 1)
+SMOOTH_CHUNKS = (4, 3, 2, 1)
+POST_CHUNKS = (4, 3, 5, 7, 2, 1)
 
 
 def sweep_scales():
@@ -161,9 +162,9 @@
     return [join_sides(parts[p], weighted(modulus[p][1], plain[p], heavy[p])) for p in range(count)]
 
 
-def sweep(planes, rows, now, later, rest, modulus, diag, inverse, scale, emit=None):
+def sweep(chunks, planes, rows, now, later, rest, modulus, diag, inverse, scale, emit=None):
     lo, hi = planes
-    chunk = next(n for n in CHUNKS if (hi - lo) % n == 0)
+    chunk = next(n for n in chunks if (hi - lo) % n == 0)
     sides = len(rest) if not emit else 1
 
     def body(i, carry):
@@ -453,7 +454,7 @@
         if k % 2 == 0:
             now, later = later, now
         rows = (0, 8, 16) if k == 1 else (4, 12)
-        sweep((2 + k, 22 - k), rows, now, later, (rest, rest_s), *readers, scales[k - 1] if k < SWEEPS else None)
+        sweep(SMOOTH_CHUNKS, (2 + k, 22 - k), rows, now, later, (rest, rest_s), *readers, scales[k - 1] if k < SWEEPS else None)
         if k < SWEEPS:
             gather(later[0], False)
 
@@ -535,7 +536,7 @@
             cmod[plane, pl.ds(18, 6), :] = above
 
     def begin(i, carry):
-        for plane in (1 + 2 * i, 2 + 2 * i):
+        for plane in [1 + 7 * i + j for j in range(7)]:
             for t in range(2):
                 here, margin = pl.ds(8 * t, 8), pl.ds(8 + 8 * t, 8)
                 mid, d, inv = ring_diagonal(cmod, plane, 8 + 8 * t)
@@ -550,7 +551,7 @@
                     cva[c, plane, margin, :] = mid * step
         return carry
 
-    lax.fori_loop(0, 7, begin, 0)
+    lax.fori_loop(0, 2, begin, 0)
 
     def gather(steps, start):
         def body(p, carry):
@@ -569,7 +570,7 @@
     coarse_moduli = [[reader(cmod, 8), reader(cprev, 0), reader(cnext, 0)]]
     for k in range(1, SWEEPS):
         now, later = ((ca, cva), (cb, cvb)) if k % 2 else ((cb, cvb), (ca, cva))
-        sweep((1 + k, 15 - k), (0, 8) if k < 3 else (4,), now, later, (crest,), coarse_moduli, [reader(cdiag, 0)], [reader(cinv, 0)], scales[k - 1])
+        sweep(POST_CHUNKS, (1 + k, 15 - k), (0, 8) if k < 3 else (4,), now, later, (crest,), coarse_moduli, [reader(cdiag, 0)], [reader(cinv, 0)], scales[k - 1])
         gather(later[0], False)
 
     for c in range(3):
@@ -638,7 +639,7 @@
         scale = scales[k - 1] if k else (None, 1.0 / THETA)
         last = k == SWEEPS - 1
         sweep(
-            (1 + k, 15 - k), (4,) if last else (0, 8), now, later, (rest, rest_s), moduli, held(1), held(2), scale,
+            POST_CHUNKS, (1 + k, 15 - k), (4,) if last else (0, 8), now, later, (rest, rest_s), moduli, held(1), held(2), scale,
             emit if last else None,
         )
         if not last:

time: 76.9 us -> 75.7 us (0.984)
  Pallas kernels: 23.5 us -> 22.2 us
    pallas_call x1, Pallas kernels: 10.4 us -> 9.16 us  [on_device(): call(post_kernel, POST_OUTS, POST_SCRATCH)]
where the time goes in v2:
time: 75.7 us; the launch traced here: 75.2 us
  starting transfers between devices  27.7 us (37%)
  waiting for transfers between devices  22.9 us (30%)
  Pallas kernels  22.2 us (29%)
  other arithmetic  1.68 us (2%)
    ppermute x5, waiting for transfers between devices, neighbours(): before = lax.ppermute(to_next, axis, [(i, i + 1) for i in range(count - 1)])  16.6 us
    ppermute x5, starting transfers between devices, neighbours(): before = lax.ppermute(to_next, axis, [(i, i + 1) for i in range(count - 1)])  15.1 us
    ppermute x5, starting transfers between devices, neighbours(): lax.ppermute(to_previous, axis, [(i + 1, i) for i in range(count - 1)])  12.6 us
    pallas_call x1, Pallas kernels, on_device(): call(smooth_kernel, SMOOTH_OUTS, SMOOTH_SCRATCH)(main, after, before)  11.9 us
    pallas_call x1, Pallas kernels, on_device(): call(post_kernel, POST_OUTS, POST_SCRATCH)  9.16 us
    ppermute x5, waiting for transfers between devices, neighbours(): lax.ppermute(to_previous, axis, [(i + 1, i) for i in range(count - 1)])  6.22 us
  transfers between devices with their start and end apart: 10, of which 10 were waited for; matrix products, arithmetic and copies ran while one was open for 0% of the time, Pallas kernels for 0%

profile of v2, /device:TPU:302, one launch (start us, length us, event | category | flops | bytes accessed | tf_op | source)
XLA Modules:
  0.0 75.2 jit_solution(7048741548943214853)
XLA Ops:
  0.6 0.8 %fusion.2 = f32[1,8,8,128]{3,2,1,0:T(8,128)S(1)} fusion(s32[8,8,128]{2,1,0:T(8,128)} %param.2), kind=kLoop, calls=%fused_computation.4 | loop fusion | flops 57344 | bytes 65536 | tf_op jit(solution)/shard_map/broadcast_in_dim | solution.py:705
  1.4 0.9 %pad_maximum_fusion.own = f32[4,8,8,128]{3,2,1,0:T(8,128)S(1)} fusion(f32[1,8,8,128]{3,2,1,0:T(8,128)S(1)} %fusion.2, f32[3,8,8,128]{3,2,1,0:T(8,128)} %param.3), kind=kLoop, calls=%fused_computation | loop fusion | flops 32768 | bytes 262144 | tf_op jit(solution)/shard_map/concatenate | solution.py:705
  2.3 1.9 %collective-permute-start = (f32[25,8,128]{2,1,0:T(8,128)S(1)}, f32[25,8,128]{2,1,0:T(8,128)S(1)}, u32[]{:S(2)}, u32[]{:S(2)}) collective-permute-start(f32[25,8,128]{2,1,0:T(8,128)S(1)} %get-tuple-element.19), channel_id=1, source_target_pairs={{64,0},{128,64},{192,128},{256,192},{320,256},{384,320},{448,384},... | collective-permute-start | bytes 307208 | tf_op jit(solution)/shard_map/ppermute | solution.py:660
  4.3 3.9 %collective-permute-start.1 = (f32[25,8,128]{2,1,0:T(8,128)S(1)}, f32[25,8,128]{2,1,0:T(8,128)S(1)}, u32[]{:S(2)}, u32[]{:S(2)}) collective-permute-start(f32[25,8,128]{2,1,0:T(8,128)S(1)} %get-tuple-element.20), channel_id=1, source_target_pairs={{0,64},{64,128},{128,192},{192,256},{256,320},{320,384},{384,448},... | collective-permute-start | bytes 307208 | tf_op jit(solution)/shard_map/ppermute | solution.py:661
  8.2 0.7 collective-permute-done.right
  8.9 3.1 %collective-permute-done.1.left = f32[25,8,128]{2,1,0:T(8,128)S(1)} collective-permute-done((f32[25,8,128]{2,1,0:T(8,128)S(1)}, f32[25,8,128]{2,1,0:T(8,128)S(1)}, u32[]{:S(2)}, u32[]{:S(2)}) %collective-permute-start.1) | collective-permute-done | bytes 102432 | tf_op jit(solution)/shard_map/ppermute | solution.py:661
  12.1 3.3 %collective-permute-start.2 = (f32[520,128]{1,0:T(8,128)S(1)}, f32[520,128]{1,0:T(8,128)S(1)}, u32[]{:S(2)}, u32[]{:S(2)}) collective-permute-start(f32[520,128]{1,0:T(8,128)S(1)} %get-tuple-element.21), channel_id=1, source_target_pairs={{8,0},{16,8},{24,16},{32,24},{40,32},{48,40},{56,48},{9,1},{17,9},... | collective-permute-start | bytes 798728 | tf_op jit(solution)/shard_map/ppermute | solution.py:660
  15.4 2.6 %collective-permute-start.3 = (f32[520,128]{1,0:T(8,128)S(1)}, f32[520,128]{1,0:T(8,128)S(1)}, u32[]{:S(2)}, u32[]{:S(2)}) collective-permute-start(f32[520,128]{1,0:T(8,128)S(1)} %get-tuple-element.22), channel_id=1, source_target_pairs={{0,8},{8,16},{16,24},{24,32},{32,40},{40,48},{48,56},{1,9},{9,17},... | collective-permute-start | bytes 798728 | tf_op jit(solution)/shard_map/ppermute | solution.py:661
  18.0 3.0 %collective-permute-done.2.up = f32[520,128]{1,0:T(8,128)S(1)} collective-permute-done((f32[520,128]{1,0:T(8,128)S(1)}, f32[520,128]{1,0:T(8,128)S(1)}, u32[]{:S(2)}, u32[]{:S(2)}) %collective-permute-start.2) | collective-permute-done | bytes 266272 | tf_op jit(solution)/shard_map/ppermute | solution.py:660
  21.0 3.0 %collective-permute-done.3.down = f32[520,128]{1,0:T(8,128)S(1)} collective-permute-done((f32[520,128]{1,0:T(8,128)S(1)}, f32[520,128]{1,0:T(8,128)S(1)}, u32[]{:S(2)}, u32[]{:S(2)}) %collective-permute-start.3) | collective-permute-done | bytes 266272 | tf_op jit(solution)/shard_map/ppermute | solution.py:661
  24.0 1.1 %shard_map.43 = (f32[4,24,24,128]{3,2,1,0:T(8,128)S(1)}, f32[12,24,128]{2,1,0:T(8,128)S(1)}, f32[12,24,128]{2,1,0:T(8,128)S(1)}) custom-call(f32[4,8,8,128]{3,2,1,0:T(8,128)S(1)} %pad_maximum_fusion.own, f32[25,8,128]{2,1,0:T(8,128)S(1)} %collective-permute-done.right, f32[25,8,128]{2,1,0:T(8,128)S(1)} %collective-permute-done.1.left, ...), custom_call_target="tpu_custom_call" | custom-call | tf_op jit(solution)/shard_map/pallas_call | solution.py:710
  25.0 1.9 %collective-permute-start.4 = (f32[12,24,128]{2,1,0:T(8,128)S(1)}, f32[12,24,128]{2,1,0:T(8,128)S(1)}, u32[]{:S(2)}, u32[]{:S(2)}) collective-permute-start(f32[12,24,128]{2,1,0:T(8,128)S(1)} %get-tuple-element.24), channel_id=1, source_target_pairs={{1,0},{2,1},{3,2},{4,3},{5,4},{6,5},{7,6},{9,8},{10,9},{11,10},{12... | collective-permute-start | bytes 442376 | tf_op jit(solution)/shard_map/ppermute | solution.py:660
  27.0 2.4 %collective-permute-start.5 = (f32[12,24,128]{2,1,0:T(8,128)S(1)}, f32[12,24,128]{2,1,0:T(8,128)S(1)}, u32[]{:S(2)}, u32[]{:S(2)}) collective-permute-start(f32[12,24,128]{2,1,0:T(8,128)S(1)} %get-tuple-element.25), channel_id=1, source_target_pairs={{0,1},{1,2},{2,3},{3,4},{4,5},{5,6},{6,7},{8,9},{9,10},{10,11},{11... | collective-permute-start | bytes 442376 | tf_op jit(solution)/shard_map/ppermute | solution.py:661
  29.6 3.8 %collective-permute-done.5.before = f32[12,24,128]{2,1,0:T(8,128)S(1)} collective-permute-done((f32[12,24,128]{2,1,0:T(8,128)S(1)}, f32[12,24,128]{2,1,0:T(8,128)S(1)}, u32[]{:S(2)}, u32[]{:S(2)}) %collective-permute-start.5) | collective-permute-done | bytes 147488 | tf_op jit(solution)/shard_map/ppermute | solution.py:661
  33.4 11.9 %shard_map.44 = (f32[3,8,8,128]{3,2,1,0:T(8,128)S(1)}, f32[4,8,8,128]{3,2,1,0:T(8,128)S(1)}, f32[192,128]{1,0:T(8,128)S(1)}, f32[192,128]{1,0:T(8,128)S(1)}, f32...) custom-call(f32[4,24,24,128]{3,2,1,0:T(8,128)S(1)} %get-tuple-elemen, ...), custom_call_target="tpu_custom_call" | custom-call | tf_op jit(solution)/shard_map/pallas_call | solution.py:712
  45.3 1.9 %collective-permute-start.6 = (f32[192,128]{1,0:T(8,128)S(1)}, f32[192,128]{1,0:T(8,128)S(1)}, u32[]{:S(2)}, u32[]{:S(2)}) collective-permute-start(f32[192,128]{1,0:T(8,128)S(1)} %get-tuple-element.27), channel_id=1, source_target_pairs={{64,0},{128,64},{192,128},{256,192},{320,256},{384,320},{448,384},... | collective-permute-start | bytes 294920 | tf_op jit(solution)/shard_map/ppermute | solution.py:660
  47.2 3.9 %collective-permute-start.7 = (f32[192,128]{1,0:T(8,128)S(1)}, f32[192,128]{1,0:T(8,128)S(1)}, u32[]{:S(2)}, u32[]{:S(2)}) collective-permute-start(f32[192,128]{1,0:T(8,128)S(1)} %get-tuple-element.28), channel_id=1, source_target_pairs={{0,64},{64,128},{128,192},{192,256},{256,320},{320,384},{384,448},... | collective-permute-start | bytes 294920 | tf_op jit(solution)/shard_map/ppermute | solution.py:661
  51.2 0.7 collective-permute-done.6.right
  51.8 3.1 %collective-permute-done.7.left = f32[192,128]{1,0:T(8,128)S(1)} collective-permute-done((f32[192,128]{1,0:T(8,128)S(1)}, f32[192,128]{1,0:T(8,128)S(1)}, u32[]{:S(2)}, u32[]{:S(2)}) %collective-permute-start.7) | collective-permute-done | bytes 98336 | tf_op jit(solution)/shard_map/ppermute | solution.py:661
  55.0 3.6 %collective-permute-start.8 = (f32[368,128]{1,0:T(8,128)S(1)}, f32[368,128]{1,0:T(8,128)S(1)}, u32[]{:S(2)}, u32[]{:S(2)}) collective-permute-start(f32[368,128]{1,0:T(8,128)S(1)} %get-tuple-element.31), channel_id=1, source_target_pairs={{8,0},{16,8},{24,16},{32,24},{40,32},{48,40},{56,48},{9,1},{17,9},... | collective-permute-start | bytes 565256 | tf_op jit(solution)/shard_map/ppermute | solution.py:660
  58.6 2.3 %collective-permute-start.9 = (f32[368,128]{1,0:T(8,128)S(1)}, f32[368,128]{1,0:T(8,128)S(1)}, u32[]{:S(2)}, u32[]{:S(2)}) collective-permute-start(f32[368,128]{1,0:T(8,128)S(1)} %get-tuple-element.32), channel_id=1, source_target_pairs={{0,8},{8,16},{16,24},{24,32},{32,40},{40,48},{48,56},{1,9},{9,17},... | collective-permute-start | bytes 565256 | tf_op jit(solution)/shard_map/ppermute | solution.py:661
  60.9 1.6 %collective-permute-done.8.up = f32[368,128]{1,0:T(8,128)S(1)} collective-permute-done((f32[368,128]{1,0:T(8,128)S(1)}, f32[368,128]{1,0:T(8,128)S(1)}, u32[]{:S(2)}, u32[]{:S(2)}) %collective-permute-start.8) | collective-permute-done | bytes 188448 | tf_op jit(solution)/shard_map/ppermute | solution.py:660
  62.5 3.6 %collective-permute-done.9.down = f32[368,128]{1,0:T(8,128)S(1)} collective-permute-done((f32[368,128]{1,0:T(8,128)S(1)}, f32[368,128]{1,0:T(8,128)S(1)}, u32[]{:S(2)}, u32[]{:S(2)}) %collective-permute-start.9) | collective-permute-done | bytes 188448 | tf_op jit(solution)/shard_map/ppermute | solution.py:661
  66.1 9.2 %shard_map.46 = (f32[3,8,8,128]{3,2,1,0:T(8,128)}, f32[3,4,4,64]{3,2,1,0:T(4,128)}) custom-call(f32[4,8,8,128]{3,2,1,0:T(8,128)S(1)} %get-tuple-element.26.own, f32[192,128]{1,0:T(8,128)S(1)} %collective-permute-done.6.right, f32[192,128]{1,0:T(8,128)S(1)} %collective-permute-done.7.left, f32[368,128]{1,0:T(8,128)S(1)} %collective-permute-done.8.up, ...), custom_call_target="tpu_custom_call" | custom-call | tf_op jit(solution)/shard_map/pallas_call | solution.py:718
  (4 shorter events, 0.4 us)
Async XLA Ops:
  2.3 6.6 %collective-permute-start = (f32[25,8,128]{2,1,0:T(8,128)S(1)}, f32[25,8,128]{2,1,0:T(8,128)S(1)}, u32[]{:S(2)}, u32[]{:S(2)}) collective-permute-start(f32[25,8,128]{2,1,0:T(8,128)S(1)} %get-tuple-element.19), channel_id=1, source_target_pairs={{64,0},{128,64},{192,128},{256,192},{320,256},{384,320},{448,384},... | collective-permute-start | bytes 307208 | tf_op jit(solution)/shard_map/ppermute | solution.py:660
  4.3 7.8 %collective-permute-start.1 = (f32[25,8,128]{2,1,0:T(8,128)S(1)}, f32[25,8,128]{2,1,0:T(8,128)S(1)}, u32[]{:S(2)}, u32[]{:S(2)}) collective-permute-start(f32[25,8,128]{2,1,0:T(8,128)S(1)} %get-tuple-element.20), channel_id=1, source_target_pairs={{0,64},{64,128},{128,192},{192,256},{256,320},{320,384},{384,448},... | collective-permute-start | bytes 307208 | tf_op jit(solution)/shard_map/ppermute | solution.py:661
  12.1 8.9 %collective-permute-start.2 = (f32[520,128]{1,0:T(8,128)S(1)}, f32[520,128]{1,0:T(8,128)S(1)}, u32[]{:S(2)}, u32[]{:S(2)}) collective-permute-start(f32[520,128]{1,0:T(8,128)S(1)} %get-tuple-element.21), channel_id=1, source_target_pairs={{8,0},{16,8},{24,16},{32,24},{40,32},{48,40},{56,48},{9,1},{17,9},... | collective-permute-start | bytes 798728 | tf_op jit(solution)/shard_map/ppermute | solution.py:660
  15.4 8.6 %collective-permute-start.3 = (f32[520,128]{1,0:T(8,128)S(1)}, f32[520,128]{1,0:T(8,128)S(1)}, u32[]{:S(2)}, u32[]{:S(2)}) collective-permute-start(f32[520,128]{1,0:T(8,128)S(1)} %get-tuple-element.22), channel_id=1, source_target_pairs={{0,8},{8,16},{16,24},{24,32},{32,40},{40,48},{48,56},{1,9},{9,17},... | collective-permute-start | bytes 798728 | tf_op jit(solution)/shard_map/ppermute | solution.py:661
  25.0 4.6 %collective-permute-start.4 = (f32[12,24,128]{2,1,0:T(8,128)S(1)}, f32[12,24,128]{2,1,0:T(8,128)S(1)}, u32[]{:S(2)}, u32[]{:S(2)}) collective-permute-start(f32[12,24,128]{2,1,0:T(8,128)S(1)} %get-tuple-element.24), channel_id=1, source_target_pairs={{1,0},{2,1},{3,2},{4,3},{5,4},{6,5},{7,6},{9,8},{10,9},{11,10},{12... | collective-permute-start | bytes 442376 | tf_op jit(solution)/shard_map/ppermute | solution.py:660
  27.0 6.5 %collective-permute-start.5 = (f32[12,24,128]{2,1,0:T(8,128)S(1)}, f32[12,24,128]{2,1,0:T(8,128)S(1)}, u32[]{:S(2)}, u32[]{:S(2)}) collective-permute-start(f32[12,24,128]{2,1,0:T(8,128)S(1)} %get-tuple-element.25), channel_id=1, source_target_pairs={{0,1},{1,2},{2,3},{3,4},{4,5},{5,6},{6,7},{8,9},{9,10},{10,11},{11... | collective-permute-start | bytes 442376 | tf_op jit(solution)/shard_map/ppermute | solution.py:661
  45.3 6.5 %collective-permute-start.6 = (f32[192,128]{1,0:T(8,128)S(1)}, f32[192,128]{1,0:T(8,128)S(1)}, u32[]{:S(2)}, u32[]{:S(2)}) collective-permute-start(f32[192,128]{1,0:T(8,128)S(1)} %get-tuple-element.27), channel_id=1, source_target_pairs={{64,0},{128,64},{192,128},{256,192},{320,256},{384,320},{448,384},... | collective-permute-start | bytes 294920 | tf_op jit(solution)/shard_map/ppermute | solution.py:660
  47.2 7.7 %collective-permute-start.7 = (f32[192,128]{1,0:T(8,128)S(1)}, f32[192,128]{1,0:T(8,128)S(1)}, u32[]{:S(2)}, u32[]{:S(2)}) collective-permute-start(f32[192,128]{1,0:T(8,128)S(1)} %get-tuple-element.28), channel_id=1, source_target_pairs={{0,64},{64,128},{128,192},{192,256},{256,320},{320,384},{384,448},... | collective-permute-start | bytes 294920 | tf_op jit(solution)/shard_map/ppermute | solution.py:661
  55.0 7.5 %collective-permute-start.8 = (f32[368,128]{1,0:T(8,128)S(1)}, f32[368,128]{1,0:T(8,128)S(1)}, u32[]{:S(2)}, u32[]{:S(2)}) collective-permute-start(f32[368,128]{1,0:T(8,128)S(1)} %get-tuple-element.31), channel_id=1, source_target_pairs={{8,0},{16,8},{24,16},{32,24},{40,32},{48,40},{56,48},{9,1},{17,9},... | collective-permute-start | bytes 565256 | tf_op jit(solution)/shard_map/ppermute | solution.py:660
  58.6 7.5 %collective-permute-start.9 = (f32[368,128]{1,0:T(8,128)S(1)}, f32[368,128]{1,0:T(8,128)S(1)}, u32[]{:S(2)}, u32[]{:S(2)}) collective-permute-start(f32[368,128]{1,0:T(8,128)S(1)} %get-tuple-element.32), channel_id=1, source_target_pairs={{0,8},{8,16},{16,24},{24,32},{32,40},{40,48},{48,56},{1,9},{9,17},... | collective-permute-start | bytes 565256 | tf_op jit(solution)/shard_map/ppermute | solution.py:661

commit v3 on v2

--- a/solution.py
+++ b/solution.py
@@ -327,7 +327,7 @@
             last[pair, pl.ds(8 * t, 8), :] = tail
         return carry
 
-    lax.fori_loop(0, 12, pack, 0, unroll=2)
+    lax.fori_loop(0, 12, pack, 0, unroll=4)
 
 
 LAYER_X = 6 * 8 + 3 * 5 * 6
@@ -403,7 +403,7 @@
                 modulus_s[plane, pl.ds(8 + 8 * t, 8), :] = jnp.where(group == 3, value, spread)
         return carry
 
-    lax.fori_loop(0, 12, place, 0, unroll=2)
+    lax.fori_loop(0, 12, place, 0, unroll=4)
 
     def begin(i, carry):
         for plane in (2 + 2 * i, 3 + 2 * i):
@@ -471,7 +471,7 @@
         pairs_s[1, p] = 0.25 * four(modulus_s, (), 8)
         return carry
 
-    lax.fori_loop(0, 8, restrict, 0, unroll=2)
+    lax.fori_loop(0, 8, restrict, 0, unroll=4)
     coarse = exact_dot(pairs[...].reshape(256, 128), pair_matrix(None, 0)).reshape(4, 8, 8, 128)
     for c in range(4):
         source = pairs_s[1 if c == 3 else 0].reshape(64, 128)
@@ -506,7 +506,7 @@
             side_state[1 + f, p] = ref_s[4 + p, pl.ds(row, 16), :]
         return carry
 
-    lax.fori_loop(0, 16, keep_state, 0, unroll=2)
+    lax.fori_loop(0, 16, keep_state, 0, unroll=4)
 
 
 def post_kernel(

time: 75.7 us -> 75 us (level)
  no operation moved by 1% of the time
where the time goes in v3:
time: 75 us; the launch traced here: 74.6 us
  starting transfers between devices  27.7 us (37%)
  waiting for transfers between devices  22.9 us (31%)
  Pallas kernels  21.6 us (29%)
  other arithmetic  1.68 us (2%)
  between operations  0.75 us (1%)
    ppermute x5, waiting for transfers between devices, neighbours(): before = lax.ppermute(to_next, axis, [(i, i + 1) for i in range(count - 1)])  16.6 us
    ppermute x5, starting transfers between devices, neighbours(): before = lax.ppermute(to_next, axis, [(i, i + 1) for i in range(count - 1)])  15.1 us
    ppermute x5, starting transfers between devices, neighbours(): lax.ppermute(to_previous, axis, [(i + 1, i) for i in range(count - 1)])  12.6 us
    pallas_call x1, Pallas kernels, on_device(): call(smooth_kernel, SMOOTH_OUTS, SMOOTH_SCRATCH)(main, after, before)  11.5 us
    pallas_call x1, Pallas kernels, on_device(): call(post_kernel, POST_OUTS, POST_SCRATCH)  9.16 us
    ppermute x5, waiting for transfers between devices, neighbours(): lax.ppermute(to_previous, axis, [(i + 1, i) for i in range(count - 1)])  6.22 us
  transfers between devices with their start and end apart: 10, of which 10 were waited for; matrix products, arithmetic and copies ran while one was open for 0% of the time, Pallas kernels for 0%

profile of v3, /device:TPU:302, one launch (start us, length us, event | category | flops | bytes accessed | tf_op | source)
XLA Modules:
  0.0 74.6 jit_solution(14329907275762654570)
XLA Ops:
  0.6 0.8 %fusion.2 = f32[1,8,8,128]{3,2,1,0:T(8,128)S(1)} fusion(s32[8,8,128]{2,1,0:T(8,128)} %param.2), kind=kLoop, calls=%fused_computation.4 | loop fusion | flops 57344 | bytes 65536 | tf_op jit(solution)/shard_map/broadcast_in_dim | solution.py:705
  1.4 0.9 %pad_maximum_fusion.own = f32[4,8,8,128]{3,2,1,0:T(8,128)S(1)} fusion(f32[1,8,8,128]{3,2,1,0:T(8,128)S(1)} %fusion.2, f32[3,8,8,128]{3,2,1,0:T(8,128)} %param.3), kind=kLoop, calls=%fused_computation | loop fusion | flops 32768 | bytes 262144 | tf_op jit(solution)/shard_map/concatenate | solution.py:705
  2.3 1.9 %collective-permute-start = (f32[25,8,128]{2,1,0:T(8,128)S(1)}, f32[25,8,128]{2,1,0:T(8,128)S(1)}, u32[]{:S(2)}, u32[]{:S(2)}) collective-permute-start(f32[25,8,128]{2,1,0:T(8,128)S(1)} %get-tuple-element.19), channel_id=1, source_target_pairs={{64,0},{128,64},{192,128},{256,192},{320,256},{384,320},{448,384},... | collective-permute-start | bytes 307208 | tf_op jit(solution)/shard_map/ppermute | solution.py:660
  4.3 3.9 %collective-permute-start.1 = (f32[25,8,128]{2,1,0:T(8,128)S(1)}, f32[25,8,128]{2,1,0:T(8,128)S(1)}, u32[]{:S(2)}, u32[]{:S(2)}) collective-permute-start(f32[25,8,128]{2,1,0:T(8,128)S(1)} %get-tuple-element.20), channel_id=1, source_target_pairs={{0,64},{64,128},{128,192},{192,256},{256,320},{320,384},{384,448},... | collective-permute-start | bytes 307208 | tf_op jit(solution)/shard_map/ppermute | solution.py:661
  8.2 0.7 collective-permute-done.right
  8.9 3.1 %collective-permute-done.1.left = f32[25,8,128]{2,1,0:T(8,128)S(1)} collective-permute-done((f32[25,8,128]{2,1,0:T(8,128)S(1)}, f32[25,8,128]{2,1,0:T(8,128)S(1)}, u32[]{:S(2)}, u32[]{:S(2)}) %collective-permute-start.1) | collective-permute-done | bytes 102432 | tf_op jit(solution)/shard_map/ppermute | solution.py:661
  12.1 3.3 %collective-permute-start.2 = (f32[520,128]{1,0:T(8,128)S(1)}, f32[520,128]{1,0:T(8,128)S(1)}, u32[]{:S(2)}, u32[]{:S(2)}) collective-permute-start(f32[520,128]{1,0:T(8,128)S(1)} %get-tuple-element.21), channel_id=1, source_target_pairs={{8,0},{16,8},{24,16},{32,24},{40,32},{48,40},{56,48},{9,1},{17,9},... | collective-permute-start | bytes 798728 | tf_op jit(solution)/shard_map/ppermute | solution.py:660
  15.4 2.6 %collective-permute-start.3 = (f32[520,128]{1,0:T(8,128)S(1)}, f32[520,128]{1,0:T(8,128)S(1)}, u32[]{:S(2)}, u32[]{:S(2)}) collective-permute-start(f32[520,128]{1,0:T(8,128)S(1)} %get-tuple-element.22), channel_id=1, source_target_pairs={{0,8},{8,16},{16,24},{24,32},{32,40},{40,48},{48,56},{1,9},{9,17},... | collective-permute-start | bytes 798728 | tf_op jit(solution)/shard_map/ppermute | solution.py:661
  18.0 3.0 %collective-permute-done.2.up = f32[520,128]{1,0:T(8,128)S(1)} collective-permute-done((f32[520,128]{1,0:T(8,128)S(1)}, f32[520,128]{1,0:T(8,128)S(1)}, u32[]{:S(2)}, u32[]{:S(2)}) %collective-permute-start.2) | collective-permute-done | bytes 266272 | tf_op jit(solution)/shard_map/ppermute | solution.py:660
  21.0 3.0 %collective-permute-done.3.down = f32[520,128]{1,0:T(8,128)S(1)} collective-permute-done((f32[520,128]{1,0:T(8,128)S(1)}, f32[520,128]{1,0:T(8,128)S(1)}, u32[]{:S(2)}, u32[]{:S(2)}) %collective-permute-start.3) | collective-permute-done | bytes 266272 | tf_op jit(solution)/shard_map/ppermute | solution.py:661
  24.0 0.9 %shard_map.43 = (f32[4,24,24,128]{3,2,1,0:T(8,128)S(1)}, f32[12,24,128]{2,1,0:T(8,128)S(1)}, f32[12,24,128]{2,1,0:T(8,128)S(1)}) custom-call(f32[4,8,8,128]{3,2,1,0:T(8,128)S(1)} %pad_maximum_fusion.own, f32[25,8,128]{2,1,0:T(8,128)S(1)} %collective-permute-done.right, f32[25,8,128]{2,1,0:T(8,128)S(1)} %collective-permute-done.1.left, ...), custom_call_target="tpu_custom_call" | custom-call | tf_op jit(solution)/shard_map/pallas_call | solution.py:710
  24.8 1.9 %collective-permute-start.4 = (f32[12,24,128]{2,1,0:T(8,128)S(1)}, f32[12,24,128]{2,1,0:T(8,128)S(1)}, u32[]{:S(2)}, u32[]{:S(2)}) collective-permute-start(f32[12,24,128]{2,1,0:T(8,128)S(1)} %get-tuple-element.24), channel_id=1, source_target_pairs={{1,0},{2,1},{3,2},{4,3},{5,4},{6,5},{7,6},{9,8},{10,9},{11,10},{12... | collective-permute-start | bytes 442376 | tf_op jit(solution)/shard_map/ppermute | solution.py:660
  26.8 2.4 %collective-permute-start.5 = (f32[12,24,128]{2,1,0:T(8,128)S(1)}, f32[12,24,128]{2,1,0:T(8,128)S(1)}, u32[]{:S(2)}, u32[]{:S(2)}) collective-permute-start(f32[12,24,128]{2,1,0:T(8,128)S(1)} %get-tuple-element.25), channel_id=1, source_target_pairs={{0,1},{1,2},{2,3},{3,4},{4,5},{5,6},{6,7},{8,9},{9,10},{10,11},{11... | collective-permute-start | bytes 442376 | tf_op jit(solution)/shard_map/ppermute | solution.py:661
  29.4 3.8 %collective-permute-done.5.before = f32[12,24,128]{2,1,0:T(8,128)S(1)} collective-permute-done((f32[12,24,128]{2,1,0:T(8,128)S(1)}, f32[12,24,128]{2,1,0:T(8,128)S(1)}, u32[]{:S(2)}, u32[]{:S(2)}) %collective-permute-start.5) | collective-permute-done | bytes 147488 | tf_op jit(solution)/shard_map/ppermute | solution.py:661
  33.2 11.5 %shard_map.44 = (f32[3,8,8,128]{3,2,1,0:T(8,128)S(1)}, f32[4,8,8,128]{3,2,1,0:T(8,128)S(1)}, f32[192,128]{1,0:T(8,128)S(1)}, f32[192,128]{1,0:T(8,128)S(1)}, f32...) custom-call(f32[4,24,24,128]{3,2,1,0:T(8,128)S(1)} %get-tuple-elemen, ...), custom_call_target="tpu_custom_call" | custom-call | tf_op jit(solution)/shard_map/pallas_call | solution.py:712
  44.7 1.9 %collective-permute-start.6 = (f32[192,128]{1,0:T(8,128)S(1)}, f32[192,128]{1,0:T(8,128)S(1)}, u32[]{:S(2)}, u32[]{:S(2)}) collective-permute-start(f32[192,128]{1,0:T(8,128)S(1)} %get-tuple-element.27), channel_id=1, source_target_pairs={{64,0},{128,64},{192,128},{256,192},{320,256},{384,320},{448,384},... | collective-permute-start | bytes 294920 | tf_op jit(solution)/shard_map/ppermute | solution.py:660
  46.6 3.9 %collective-permute-start.7 = (f32[192,128]{1,0:T(8,128)S(1)}, f32[192,128]{1,0:T(8,128)S(1)}, u32[]{:S(2)}, u32[]{:S(2)}) collective-permute-start(f32[192,128]{1,0:T(8,128)S(1)} %get-tuple-element.28), channel_id=1, source_target_pairs={{0,64},{64,128},{128,192},{192,256},{256,320},{320,384},{384,448},... | collective-permute-start | bytes 294920 | tf_op jit(solution)/shard_map/ppermute | solution.py:661
  50.5 0.7 collective-permute-done.6.right
  51.2 3.1 %collective-permute-done.7.left = f32[192,128]{1,0:T(8,128)S(1)} collective-permute-done((f32[192,128]{1,0:T(8,128)S(1)}, f32[192,128]{1,0:T(8,128)S(1)}, u32[]{:S(2)}, u32[]{:S(2)}) %collective-permute-start.7) | collective-permute-done | bytes 98336 | tf_op jit(solution)/shard_map/ppermute | solution.py:661
  54.4 3.6 %collective-permute-start.8 = (f32[368,128]{1,0:T(8,128)S(1)}, f32[368,128]{1,0:T(8,128)S(1)}, u32[]{:S(2)}, u32[]{:S(2)}) collective-permute-start(f32[368,128]{1,0:T(8,128)S(1)} %get-tuple-element.31), channel_id=1, source_target_pairs={{8,0},{16,8},{24,16},{32,24},{40,32},{48,40},{56,48},{9,1},{17,9},... | collective-permute-start | bytes 565256 | tf_op jit(solution)/shard_map/ppermute | solution.py:660
  58.0 2.3 %collective-permute-start.9 = (f32[368,128]{1,0:T(8,128)S(1)}, f32[368,128]{1,0:T(8,128)S(1)}, u32[]{:S(2)}, u32[]{:S(2)}) collective-permute-start(f32[368,128]{1,0:T(8,128)S(1)} %get-tuple-element.32), channel_id=1, source_target_pairs={{0,8},{8,16},{16,24},{24,32},{32,40},{40,48},{48,56},{1,9},{9,17},... | collective-permute-start | bytes 565256 | tf_op jit(solution)/shard_map/ppermute | solution.py:661
  60.2 1.6 %collective-permute-done.8.up = f32[368,128]{1,0:T(8,128)S(1)} collective-permute-done((f32[368,128]{1,0:T(8,128)S(1)}, f32[368,128]{1,0:T(8,128)S(1)}, u32[]{:S(2)}, u32[]{:S(2)}) %collective-permute-start.8) | collective-permute-done | bytes 188448 | tf_op jit(solution)/shard_map/ppermute | solution.py:660
  61.9 3.6 %collective-permute-done.9.down = f32[368,128]{1,0:T(8,128)S(1)} collective-permute-done((f32[368,128]{1,0:T(8,128)S(1)}, f32[368,128]{1,0:T(8,128)S(1)}, u32[]{:S(2)}, u32[]{:S(2)}) %collective-permute-start.9) | collective-permute-done | bytes 188448 | tf_op jit(solution)/shard_map/ppermute | solution.py:661
  65.4 9.2 %shard_map.46 = (f32[3,8,8,128]{3,2,1,0:T(8,128)}, f32[3,4,4,64]{3,2,1,0:T(4,128)}) custom-call(f32[4,8,8,128]{3,2,1,0:T(8,128)S(1)} %get-tuple-element.26.own, f32[192,128]{1,0:T(8,128)S(1)} %collective-permute-done.6.right, f32[192,128]{1,0:T(8,128)S(1)} %collective-permute-done.7.left, f32[368,128]{1,0:T(8,128)S(1)} %collective-permute-done.8.up, ...), custom_call_target="tpu_custom_call" | custom-call | tf_op jit(solution)/shard_map/pallas_call | solution.py:718
  (4 shorter events, 0.4 us)
Async XLA Ops:
  2.3 6.6 %collective-permute-start = (f32[25,8,128]{2,1,0:T(8,128)S(1)}, f32[25,8,128]{2,1,0:T(8,128)S(1)}, u32[]{:S(2)}, u32[]{:S(2)}) collective-permute-start(f32[25,8,128]{2,1,0:T(8,128)S(1)} %get-tuple-element.19), channel_id=1, source_target_pairs={{64,0},{128,64},{192,128},{256,192},{320,256},{384,320},{448,384},... | collective-permute-start | bytes 307208 | tf_op jit(solution)/shard_map/ppermute | solution.py:660
  4.3 7.8 %collective-permute-start.1 = (f32[25,8,128]{2,1,0:T(8,128)S(1)}, f32[25,8,128]{2,1,0:T(8,128)S(1)}, u32[]{:S(2)}, u32[]{:S(2)}) collective-permute-start(f32[25,8,128]{2,1,0:T(8,128)S(1)} %get-tuple-element.20), channel_id=1, source_target_pairs={{0,64},{64,128},{128,192},{192,256},{256,320},{320,384},{384,448},... | collective-permute-start | bytes 307208 | tf_op jit(solution)/shard_map/ppermute | solution.py:661
  12.1 8.9 %collective-permute-start.2 = (f32[520,128]{1,0:T(8,128)S(1)}, f32[520,128]{1,0:T(8,128)S(1)}, u32[]{:S(2)}, u32[]{:S(2)}) collective-permute-start(f32[520,128]{1,0:T(8,128)S(1)} %get-tuple-element.21), channel_id=1, source_target_pairs={{8,0},{16,8},{24,16},{32,24},{40,32},{48,40},{56,48},{9,1},{17,9},... | collective-permute-start | bytes 798728 | tf_op jit(solution)/shard_map/ppermute | solution.py:660
  15.4 8.6 %collective-permute-start.3 = (f32[520,128]{1,0:T(8,128)S(1)}, f32[520,128]{1,0:T(8,128)S(1)}, u32[]{:S(2)}, u32[]{:S(2)}) collective-permute-start(f32[520,128]{1,0:T(8,128)S(1)} %get-tuple-element.22), channel_id=1, source_target_pairs={{0,8},{8,16},{16,24},{24,32},{32,40},{40,48},{48,56},{1,9},{9,17},... | collective-permute-start | bytes 798728 | tf_op jit(solution)/shard_map/ppermute | solution.py:661
  24.8 4.6 %collective-permute-start.4 = (f32[12,24,128]{2,1,0:T(8,128)S(1)}, f32[12,24,128]{2,1,0:T(8,128)S(1)}, u32[]{:S(2)}, u32[]{:S(2)}) collective-permute-start(f32[12,24,128]{2,1,0:T(8,128)S(1)} %get-tuple-element.24), channel_id=1, source_target_pairs={{1,0},{2,1},{3,2},{4,3},{5,4},{6,5},{7,6},{9,8},{10,9},{11,10},{12... | collective-permute-start | bytes 442376 | tf_op jit(solution)/shard_map/ppermute | solution.py:660
  26.8 6.5 %collective-permute-start.5 = (f32[12,24,128]{2,1,0:T(8,128)S(1)}, f32[12,24,128]{2,1,0:T(8,128)S(1)}, u32[]{:S(2)}, u32[]{:S(2)}) collective-permute-start(f32[12,24,128]{2,1,0:T(8,128)S(1)} %get-tuple-element.25), channel_id=1, source_target_pairs={{0,1},{1,2},{2,3},{3,4},{4,5},{5,6},{6,7},{8,9},{9,10},{10,11},{11... | collective-permute-start | bytes 442376 | tf_op jit(solution)/shard_map/ppermute | solution.py:661
  44.7 6.5 %collective-permute-start.6 = (f32[192,128]{1,0:T(8,128)S(1)}, f32[192,128]{1,0:T(8,128)S(1)}, u32[]{:S(2)}, u32[]{:S(2)}) collective-permute-start(f32[192,128]{1,0:T(8,128)S(1)} %get-tuple-element.27), channel_id=1, source_target_pairs={{64,0},{128,64},{192,128},{256,192},{320,256},{384,320},{448,384},... | collective-permute-start | bytes 294920 | tf_op jit(solution)/shard_map/ppermute | solution.py:660
  46.6 7.7 %collective-permute-start.7 = (f32[192,128]{1,0:T(8,128)S(1)}, f32[192,128]{1,0:T(8,128)S(1)}, u32[]{:S(2)}, u32[]{:S(2)}) collective-permute-start(f32[192,128]{1,0:T(8,128)S(1)} %get-tuple-element.28), channel_id=1, source_target_pairs={{0,64},{64,128},{128,192},{192,256},{256,320},{320,384},{384,448},... | collective-permute-start | bytes 294920 | tf_op jit(solution)/shard_map/ppermute | solution.py:661
  54.4 7.5 %collective-permute-start.8 = (f32[368,128]{1,0:T(8,128)S(1)}, f32[368,128]{1,0:T(8,128)S(1)}, u32[]{:S(2)}, u32[]{:S(2)}) collective-permute-start(f32[368,128]{1,0:T(8,128)S(1)} %get-tuple-element.31), channel_id=1, source_target_pairs={{8,0},{16,8},{24,16},{32,24},{40,32},{48,40},{56,48},{9,1},{17,9},... | collective-permute-start | bytes 565256 | tf_op jit(solution)/shard_map/ppermute | solution.py:660
  58.0 7.5 %collective-permute-start.9 = (f32[368,128]{1,0:T(8,128)S(1)}, f32[368,128]{1,0:T(8,128)S(1)}, u32[]{:S(2)}, u32[]{:S(2)}) collective-permute-start(f32[368,128]{1,0:T(8,128)S(1)} %get-tuple-element.32), channel_id=1, source_target_pairs={{0,8},{8,16},{16,24},{24,32},{32,40},{40,48},{48,56},{1,9},{9,17},... | collective-permute-start | bytes 565256 | tf_op jit(solution)/shard_map/ppermute | solution.py:661

commit v4 on v3

--- a/solution.py
+++ b/solution.py
@@ -310,24 +310,22 @@
         main[c, plane, pl.ds(8, 8), :] = source[index]
         main[c, plane, pl.ds(8 - count, count), :] = down[pl.ds(base, count), :]
         main[c, plane, pl.ds(16, count), :] = up[pl.ds(base, count), :]
-    lane = lane_index()
+    group, lower = lane_index() // 32, lane_index() % 32 < HALO
 
     def pack(pair, carry):
         for t in range(3):
-            head = jnp.zeros((8, 128), jnp.float32)
-            tail = head
+            ends = []
             for s in range(2):
-                for c in range(4):
-                    value, place = main[c, 2 * pair + s, pl.ds(8 * t, 8), :], 32 * c + HALO * s
-                    mine = (lane >= place) & (lane < place + HALO)
-                    head = jnp.where(mine, pltpu.roll(value, place, 1) if place else value, head)
-                    turn = (place + HALO) % 128
-                    tail = jnp.where(mine, pltpu.roll(value, turn, 1) if turn else value, tail)
-            first[pair, pl.ds(8 * t, 8), :] = head
-            last[pair, pl.ds(8 * t, 8), :] = tail
-        return carry
-
-    lax.fori_loop(0, 12, pack, 0, unroll=4)
+                value = pltpu.roll(main[3, 2 * pair + s, pl.ds(8 * t, 8), :], 96 + HALO, 1)
+                for c in range(3):
+                    turned = pltpu.roll(main[c, 2 * pair + s, pl.ds(8 * t, 8), :], 32 * c + HALO, 1)
+                    value = jnp.where(group == c, turned, value)
+                ends.append(value)
+            first[pair, pl.ds(8 * t, 8), :] = jnp.where(lower, pltpu.roll(ends[0], 128 - HALO, 1), ends[1])
+            last[pair, pl.ds(8 * t, 8), :] = jnp.where(lower, ends[0], pltpu.roll(ends[1], HALO, 1))
+        return carry
+
+    lax.fori_loop(0, 12, pack, 0, unroll=6)
 
 
 LAYER_X = 6 * 8 + 3 * 5 * 6
@@ -471,7 +469,7 @@
         pairs_s[1, p] = 0.25 * four(modulus_s, (), 8)
         return carry
 
-    lax.fori_loop(0, 8, restrict, 0, unroll=4)
+    lax.fori_loop(0, 8, restrict, 0, unroll=8)
     coarse = exact_dot(pairs[...].reshape(256, 128), pair_matrix(None, 0)).reshape(4, 8, 8, 128)
     for c in range(4):
         source = pairs_s[1 if c == 3 else 0].reshape(64, 128)
@@ -506,7 +504,7 @@
             side_state[1 + f, p] = ref_s[4 + p, pl.ds(row, 16), :]
         return carry
 
-    lax.fori_loop(0, 16, keep_state, 0, unroll=4)
+    lax.fori_loop(0, 16, keep_state, 0, unroll=8)
 
 
 def post_kernel(
@@ -592,7 +590,7 @@
                 usa[2 * p + dx, pl.ds(8 + dy, 8, stride=2), :] = wide_s[p]
         return carry
 
-    lax.fori_loop(0, 8, lift, 0, unroll=2)
+    lax.fori_loop(0, 8, lift, 0, unroll=4)
 
     def weigh(p, carry):
         for c in range(3):
@@ -602,7 +600,7 @@
         rest_s[p] = side_in[0, p]
         return carry
 
-    lax.fori_loop(0, 16, weigh, 0, unroll=2)
+    lax.fori_loop(0, 16, weigh, 0, unroll=4)
     for f, target in enumerate([rest.at[c] for c in range(3)] + [rest_s]):
         target[1, pl.ds(2, 12), :] = left[pl.ds(LAYER_X + 12 * f, 12), :]
         target[14, pl.ds(2, 12), :] = right[pl.ds(LAYER_X + 12 * f, 12), :]

time: 75 us -> 75.5 us (level)
  the two profiles are of different devices: /device:TPU:302 before, /device:TPU:300 now
where the time goes in v4:
time: 75.5 us; the launch traced here: 75.1 us
  starting transfers between devices  27.7 us (37%)
  waiting for transfers between devices  22.9 us (30%)
  Pallas kernels  22.1 us (29%)
  other arithmetic  1.68 us (2%)
    ppermute x5, waiting for transfers between devices, neighbours(): before = lax.ppermute(to_next, axis, [(i, i + 1) for i in range(count - 1)])  16.6 us
    ppermute x5, starting transfers between devices, neighbours(): before = lax.ppermute(to_next, axis, [(i, i + 1) for i in range(count - 1)])  15.1 us
    ppermute x5, starting transfers between devices, neighbours(): lax.ppermute(to_previous, axis, [(i + 1, i) for i in range(count - 1)])  12.6 us
    pallas_call x1, Pallas kernels, on_device(): call(smooth_kernel, SMOOTH_OUTS, SMOOTH_SCRATCH)(main, after, before)  11.4 us
    pallas_call x1, Pallas kernels, on_device(): call(post_kernel, POST_OUTS, POST_SCRATCH)  9.15 us
    ppermute x5, waiting for transfers between devices, neighbours(): lax.ppermute(to_previous, axis, [(i + 1, i) for i in range(count - 1)])  6.22 us
  transfers between devices with their start and end apart: 10, of which 10 were waited for; matrix products, arithmetic and copies ran while one was open for 0% of the time, Pallas kernels for 0%

profile of v4, /device:TPU:300, one launch (start us, length us, event | category | flops | bytes accessed | tf_op | source)
XLA Modules:
  0.0 75.1 jit_solution(13445121173589999345)
XLA Ops:
  0.6 0.8 %fusion.2 = f32[1,8,8,128]{3,2,1,0:T(8,128)S(1)} fusion(s32[8,8,128]{2,1,0:T(8,128)} %param.2), kind=kLoop, calls=%fused_computation.4 | loop fusion | flops 57344 | bytes 65536 | tf_op jit(solution)/shard_map/broadcast_in_dim | solution.py:703
  1.4 0.9 %pad_maximum_fusion.own = f32[4,8,8,128]{3,2,1,0:T(8,128)S(1)} fusion(f32[1,8,8,128]{3,2,1,0:T(8,128)S(1)} %fusion.2, f32[3,8,8,128]{3,2,1,0:T(8,128)} %param.3), kind=kLoop, calls=%fused_computation | loop fusion | flops 32768 | bytes 262144 | tf_op jit(solution)/shard_map/concatenate | solution.py:703
  2.3 1.9 %collective-permute-start = (f32[25,8,128]{2,1,0:T(8,128)S(1)}, f32[25,8,128]{2,1,0:T(8,128)S(1)}, u32[]{:S(2)}, u32[]{:S(2)}) collective-permute-start(f32[25,8,128]{2,1,0:T(8,128)S(1)} %get-tuple-element.19), channel_id=1, source_target_pairs={{64,0},{128,64},{192,128},{256,192},{320,256},{384,320},{448,384},... | collective-permute-start | bytes 307208 | tf_op jit(solution)/shard_map/ppermute | solution.py:658
  4.3 3.9 %collective-permute-start.1 = (f32[25,8,128]{2,1,0:T(8,128)S(1)}, f32[25,8,128]{2,1,0:T(8,128)S(1)}, u32[]{:S(2)}, u32[]{:S(2)}) collective-permute-start(f32[25,8,128]{2,1,0:T(8,128)S(1)} %get-tuple-element.20), channel_id=1, source_target_pairs={{0,64},{64,128},{128,192},{192,256},{256,320},{320,384},{384,448},... | collective-permute-start | bytes 307208 | tf_op jit(solution)/shard_map/ppermute | solution.py:659
  8.2 0.7 collective-permute-done.right
  8.9 3.1 %collective-permute-done.1.left = f32[25,8,128]{2,1,0:T(8,128)S(1)} collective-permute-done((f32[25,8,128]{2,1,0:T(8,128)S(1)}, f32[25,8,128]{2,1,0:T(8,128)S(1)}, u32[]{:S(2)}, u32[]{:S(2)}) %collective-permute-start.1) | collective-permute-done | bytes 102432 | tf_op jit(solution)/shard_map/ppermute | solution.py:659
  12.1 3.3 %collective-permute-start.2 = (f32[520,128]{1,0:T(8,128)S(1)}, f32[520,128]{1,0:T(8,128)S(1)}, u32[]{:S(2)}, u32[]{:S(2)}) collective-permute-start(f32[520,128]{1,0:T(8,128)S(1)} %get-tuple-element.21), channel_id=1, source_target_pairs={{8,0},{16,8},{24,16},{32,24},{40,32},{48,40},{56,48},{9,1},{17,9},... | collective-permute-start | bytes 798728 | tf_op jit(solution)/shard_map/ppermute | solution.py:658
  15.4 2.6 %collective-permute-start.3 = (f32[520,128]{1,0:T(8,128)S(1)}, f32[520,128]{1,0:T(8,128)S(1)}, u32[]{:S(2)}, u32[]{:S(2)}) collective-permute-start(f32[520,128]{1,0:T(8,128)S(1)} %get-tuple-element.22), channel_id=1, source_target_pairs={{0,8},{8,16},{16,24},{24,32},{32,40},{40,48},{48,56},{1,9},{9,17},... | collective-permute-start | bytes 798728 | tf_op jit(solution)/shard_map/ppermute | solution.py:659
  18.0 3.0 %collective-permute-done.2.up = f32[520,128]{1,0:T(8,128)S(1)} collective-permute-done((f32[520,128]{1,0:T(8,128)S(1)}, f32[520,128]{1,0:T(8,128)S(1)}, u32[]{:S(2)}, u32[]{:S(2)}) %collective-permute-start.2) | collective-permute-done | bytes 266272 | tf_op jit(solution)/shard_map/ppermute | solution.py:658
  21.0 3.0 %collective-permute-done.3.down = f32[520,128]{1,0:T(8,128)S(1)} collective-permute-done((f32[520,128]{1,0:T(8,128)S(1)}, f32[520,128]{1,0:T(8,128)S(1)}, u32[]{:S(2)}, u32[]{:S(2)}) %collective-permute-start.3) | collective-permute-done | bytes 266272 | tf_op jit(solution)/shard_map/ppermute | solution.py:659
  24.0 1.4 %shard_map.43 = (f32[4,24,24,128]{3,2,1,0:T(8,128)S(1)}, f32[12,24,128]{2,1,0:T(8,128)S(1)}, f32[12,24,128]{2,1,0:T(8,128)S(1)}) custom-call(f32[4,8,8,128]{3,2,1,0:T(8,128)S(1)} %pad_maximum_fusion.own, f32[25,8,128]{2,1,0:T(8,128)S(1)} %collective-permute-done.right, f32[25,8,128]{2,1,0:T(8,128)S(1)} %collective-permute-done.1.left, ...), custom_call_target="tpu_custom_call" | custom-call | tf_op jit(solution)/shard_map/pallas_call | solution.py:708
  25.3 1.9 %collective-permute-start.4 = (f32[12,24,128]{2,1,0:T(8,128)S(1)}, f32[12,24,128]{2,1,0:T(8,128)S(1)}, u32[]{:S(2)}, u32[]{:S(2)}) collective-permute-start(f32[12,24,128]{2,1,0:T(8,128)S(1)} %get-tuple-element.24), channel_id=1, source_target_pairs={{1,0},{2,1},{3,2},{4,3},{5,4},{6,5},{7,6},{9,8},{10,9},{11,10},{12... | collective-permute-start | bytes 442376 | tf_op jit(solution)/shard_map/ppermute | solution.py:658
  27.3 2.4 %collective-permute-start.5 = (f32[12,24,128]{2,1,0:T(8,128)S(1)}, f32[12,24,128]{2,1,0:T(8,128)S(1)}, u32[]{:S(2)}, u32[]{:S(2)}) collective-permute-start(f32[12,24,128]{2,1,0:T(8,128)S(1)} %get-tuple-element.25), channel_id=1, source_target_pairs={{0,1},{1,2},{2,3},{3,4},{4,5},{5,6},{6,7},{8,9},{9,10},{10,11},{11... | collective-permute-start | bytes 442376 | tf_op jit(solution)/shard_map/ppermute | solution.py:659
  29.9 3.8 %collective-permute-done.5.before = f32[12,24,128]{2,1,0:T(8,128)S(1)} collective-permute-done((f32[12,24,128]{2,1,0:T(8,128)S(1)}, f32[12,24,128]{2,1,0:T(8,128)S(1)}, u32[]{:S(2)}, u32[]{:S(2)}) %collective-permute-start.5) | collective-permute-done | bytes 147488 | tf_op jit(solution)/shard_map/ppermute | solution.py:659
  33.7 11.4 %shard_map.44 = (f32[3,8,8,128]{3,2,1,0:T(8,128)S(1)}, f32[4,8,8,128]{3,2,1,0:T(8,128)S(1)}, f32[192,128]{1,0:T(8,128)S(1)}, f32[192,128]{1,0:T(8,128)S(1)}, f32...) custom-call(f32[4,24,24,128]{3,2,1,0:T(8,128)S(1)} %get-tuple-elemen, ...), custom_call_target="tpu_custom_call" | custom-call | tf_op jit(solution)/shard_map/pallas_call | solution.py:710
  45.2 1.9 %collective-permute-start.6 = (f32[192,128]{1,0:T(8,128)S(1)}, f32[192,128]{1,0:T(8,128)S(1)}, u32[]{:S(2)}, u32[]{:S(2)}) collective-permute-start(f32[192,128]{1,0:T(8,128)S(1)} %get-tuple-element.27), channel_id=1, source_target_pairs={{64,0},{128,64},{192,128},{256,192},{320,256},{384,320},{448,384},... | collective-permute-start | bytes 294920 | tf_op jit(solution)/shard_map/ppermute | solution.py:658
  47.1 3.9 %collective-permute-start.7 = (f32[192,128]{1,0:T(8,128)S(1)}, f32[192,128]{1,0:T(8,128)S(1)}, u32[]{:S(2)}, u32[]{:S(2)}) collective-permute-start(f32[192,128]{1,0:T(8,128)S(1)} %get-tuple-element.28), channel_id=1, source_target_pairs={{0,64},{64,128},{128,192},{192,256},{256,320},{320,384},{384,448},... | collective-permute-start | bytes 294920 | tf_op jit(solution)/shard_map/ppermute | solution.py:659
  51.0 0.7 collective-permute-done.6.right
  51.7 3.1 %collective-permute-done.7.left = f32[192,128]{1,0:T(8,128)S(1)} collective-permute-done((f32[192,128]{1,0:T(8,128)S(1)}, f32[192,128]{1,0:T(8,128)S(1)}, u32[]{:S(2)}, u32[]{:S(2)}) %collective-permute-start.7) | collective-permute-done | bytes 98336 | tf_op jit(solution)/shard_map/ppermute | solution.py:659
  54.9 3.6 %collective-permute-start.8 = (f32[368,128]{1,0:T(8,128)S(1)}, f32[368,128]{1,0:T(8,128)S(1)}, u32[]{:S(2)}, u32[]{:S(2)}) collective-permute-start(f32[368,128]{1,0:T(8,128)S(1)} %get-tuple-element.31), channel_id=1, source_target_pairs={{8,0},{16,8},{24,16},{32,24},{40,32},{48,40},{56,48},{9,1},{17,9},... | collective-permute-start | bytes 565256 | tf_op jit(solution)/shard_map/ppermute | solution.py:658
  58.5 2.3 %collective-permute-start.9 = (f32[368,128]{1,0:T(8,128)S(1)}, f32[368,128]{1,0:T(8,128)S(1)}, u32[]{:S(2)}, u32[]{:S(2)}) collective-permute-start(f32[368,128]{1,0:T(8,128)S(1)} %get-tuple-element.32), channel_id=1, source_target_pairs={{0,8},{8,16},{16,24},{24,32},{32,40},{40,48},{48,56},{1,9},{9,17},... | collective-permute-start | bytes 565256 | tf_op jit(solution)/shard_map/ppermute | solution.py:659
  60.7 1.6 %collective-permute-done.8.up = f32[368,128]{1,0:T(8,128)S(1)} collective-permute-done((f32[368,128]{1,0:T(8,128)S(1)}, f32[368,128]{1,0:T(8,128)S(1)}, u32[]{:S(2)}, u32[]{:S(2)}) %collective-permute-start.8) | collective-permute-done | bytes 188448 | tf_op jit(solution)/shard_map/ppermute | solution.py:658
  62.4 3.6 %collective-permute-done.9.down = f32[368,128]{1,0:T(8,128)S(1)} collective-permute-done((f32[368,128]{1,0:T(8,128)S(1)}, f32[368,128]{1,0:T(8,128)S(1)}, u32[]{:S(2)}, u32[]{:S(2)}) %collective-permute-start.9) | collective-permute-done | bytes 188448 | tf_op jit(solution)/shard_map/ppermute | solution.py:659
  65.9 9.2 %shard_map.46 = (f32[3,8,8,128]{3,2,1,0:T(8,128)}, f32[3,4,4,64]{3,2,1,0:T(4,128)}) custom-call(f32[4,8,8,128]{3,2,1,0:T(8,128)S(1)} %get-tuple-element.26.own, f32[192,128]{1,0:T(8,128)S(1)} %collective-permute-done.6.right, f32[192,128]{1,0:T(8,128)S(1)} %collective-permute-done.7.left, f32[368,128]{1,0:T(8,128)S(1)} %collective-permute-done.8.up, ...), custom_call_target="tpu_custom_call" | custom-call | tf_op jit(solution)/shard_map/pallas_call | solution.py:716
  (4 shorter events, 0.4 us)
Async XLA Ops:
  2.3 6.6 %collective-permute-start = (f32[25,8,128]{2,1,0:T(8,128)S(1)}, f32[25,8,128]{2,1,0:T(8,128)S(1)}, u32[]{:S(2)}, u32[]{:S(2)}) collective-permute-start(f32[25,8,128]{2,1,0:T(8,128)S(1)} %get-tuple-element.19), channel_id=1, source_target_pairs={{64,0},{128,64},{192,128},{256,192},{320,256},{384,320},{448,384},... | collective-permute-start | bytes 307208 | tf_op jit(solution)/shard_map/ppermute | solution.py:658
  4.3 7.8 %collective-permute-start.1 = (f32[25,8,128]{2,1,0:T(8,128)S(1)}, f32[25,8,128]{2,1,0:T(8,128)S(1)}, u32[]{:S(2)}, u32[]{:S(2)}) collective-permute-start(f32[25,8,128]{2,1,0:T(8,128)S(1)} %get-tuple-element.20), channel_id=1, source_target_pairs={{0,64},{64,128},{128,192},{192,256},{256,320},{320,384},{384,448},... | collective-permute-start | bytes 307208 | tf_op jit(solution)/shard_map/ppermute | solution.py:659
  12.1 8.9 %collective-permute-start.2 = (f32[520,128]{1,0:T(8,128)S(1)}, f32[520,128]{1,0:T(8,128)S(1)}, u32[]{:S(2)}, u32[]{:S(2)}) collective-permute-start(f32[520,128]{1,0:T(8,128)S(1)} %get-tuple-element.21), channel_id=1, source_target_pairs={{8,0},{16,8},{24,16},{32,24},{40,32},{48,40},{56,48},{9,1},{17,9},... | collective-permute-start | bytes 798728 | tf_op jit(solution)/shard_map/ppermute | solution.py:658
  15.4 8.6 %collective-permute-start.3 = (f32[520,128]{1,0:T(8,128)S(1)}, f32[520,128]{1,0:T(8,128)S(1)}, u32[]{:S(2)}, u32[]{:S(2)}) collective-permute-start(f32[520,128]{1,0:T(8,128)S(1)} %get-tuple-element.22), channel_id=1, source_target_pairs={{0,8},{8,16},{16,24},{24,32},{32,40},{40,48},{48,56},{1,9},{9,17},... | collective-permute-start | bytes 798728 | tf_op jit(solution)/shard_map/ppermute | solution.py:659
  25.3 4.6 %collective-permute-start.4 = (f32[12,24,128]{2,1,0:T(8,128)S(1)}, f32[12,24,128]{2,1,0:T(8,128)S(1)}, u32[]{:S(2)}, u32[]{:S(2)}) collective-permute-start(f32[12,24,128]{2,1,0:T(8,128)S(1)} %get-tuple-element.24), channel_id=1, source_target_pairs={{1,0},{2,1},{3,2},{4,3},{5,4},{6,5},{7,6},{9,8},{10,9},{11,10},{12... | collective-permute-start | bytes 442376 | tf_op jit(solution)/shard_map/ppermute | solution.py:658
  27.3 6.5 %collective-permute-start.5 = (f32[12,24,128]{2,1,0:T(8,128)S(1)}, f32[12,24,128]{2,1,0:T(8,128)S(1)}, u32[]{:S(2)}, u32[]{:S(2)}) collective-permute-start(f32[12,24,128]{2,1,0:T(8,128)S(1)} %get-tuple-element.25), channel_id=1, source_target_pairs={{0,1},{1,2},{2,3},{3,4},{4,5},{5,6},{6,7},{8,9},{9,10},{10,11},{11... | collective-permute-start | bytes 442376 | tf_op jit(solution)/shard_map/ppermute | solution.py:659
  45.2 6.5 %collective-permute-start.6 = (f32[192,128]{1,0:T(8,128)S(1)}, f32[192,128]{1,0:T(8,128)S(1)}, u32[]{:S(2)}, u32[]{:S(2)}) collective-permute-start(f32[192,128]{1,0:T(8,128)S(1)} %get-tuple-element.27), channel_id=1, source_target_pairs={{64,0},{128,64},{192,128},{256,192},{320,256},{384,320},{448,384},... | collective-permute-start | bytes 294920 | tf_op jit(solution)/shard_map/ppermute | solution.py:658
  47.1 7.7 %collective-permute-start.7 = (f32[192,128]{1,0:T(8,128)S(1)}, f32[192,128]{1,0:T(8,128)S(1)}, u32[]{:S(2)}, u32[]{:S(2)}) collective-permute-start(f32[192,128]{1,0:T(8,128)S(1)} %get-tuple-element.28), channel_id=1, source_target_pairs={{0,64},{64,128},{128,192},{192,256},{256,320},{320,384},{384,448},... | collective-permute-start | bytes 294920 | tf_op jit(solution)/shard_map/ppermute | solution.py:659
  54.9 7.5 %collective-permute-start.8 = (f32[368,128]{1,0:T(8,128)S(1)}, f32[368,128]{1,0:T(8,128)S(1)}, u32[]{:S(2)}, u32[]{:S(2)}) collective-permute-start(f32[368,128]{1,0:T(8,128)S(1)} %get-tuple-element.31), channel_id=1, source_target_pairs={{8,0},{16,8},{24,16},{32,24},{40,32},{48,40},{56,48},{9,1},{17,9},... | collective-permute-start | bytes 565256 | tf_op jit(solution)/shard_map/ppermute | solution.py:658
  58.5 7.5 %collective-permute-start.9 = (f32[368,128]{1,0:T(8,128)S(1)}, f32[368,128]{1,0:T(8,128)S(1)}, u32[]{:S(2)}, u32[]{:S(2)}) collective-permute-start(f32[368,128]{1,0:T(8,128)S(1)} %get-tuple-element.32), channel_id=1, source_target_pairs={{0,8},{8,16},{16,24},{24,32},{32,40},{40,48},{48,56},{1,9},{9,17},... | collective-permute-start | bytes 565256 | tf_op jit(solution)/shard_map/ppermute | solution.py:659

commit v5 on v3

--- a/solution.py
+++ b/solution.py
@@ -327,7 +327,7 @@
             last[pair, pl.ds(8 * t, 8), :] = tail
         return carry
 
-    lax.fori_loop(0, 12, pack, 0, unroll=4)
+    lax.fori_loop(0, 12, pack, 0, unroll=6)
 
 
 LAYER_X = 6 * 8 + 3 * 5 * 6
@@ -471,7 +471,7 @@
         pairs_s[1, p] = 0.25 * four(modulus_s, (), 8)
         return carry
 
-    lax.fori_loop(0, 8, restrict, 0, unroll=4)
+    lax.fori_loop(0, 8, restrict, 0, unroll=8)
     coarse = exact_dot(pairs[...].reshape(256, 128), pair_matrix(None, 0)).reshape(4, 8, 8, 128)
     for c in range(4):
         source = pairs_s[1 if c == 3 else 0].reshape(64, 128)
@@ -506,7 +506,7 @@
             side_state[1 + f, p] = ref_s[4 + p, pl.ds(row, 16), :]
         return carry
 
-    lax.fori_loop(0, 16, keep_state, 0, unroll=4)
+    lax.fori_loop(0, 16, keep_state, 0, unroll=8)
 
 
 def post_kernel(

time: 75 us -> 75 us (level)
  no operation moved by 1% of the time
where the time goes in v5:
time: 75 us; the launch traced here: 74.5 us
  starting transfers between devices  27.7 us (37%)
  waiting for transfers between devices  22.9 us (31%)
  Pallas kernels  21.5 us (29%)
  other arithmetic  1.68 us (2%)
  between operations  0.75 us (1%)
    ppermute x5, waiting for transfers between devices, neighbours(): before = lax.ppermute(to_next, axis, [(i, i + 1) for i in range(count - 1)])  16.6 us
    ppermute x5, starting transfers between devices, neighbours(): before = lax.ppermute(to_next, axis, [(i, i + 1) for i in range(count - 1)])  15.1 us
    ppermute x5, starting transfers between devices, neighbours(): lax.ppermute(to_previous, axis, [(i + 1, i) for i in range(count - 1)])  12.6 us
    pallas_call x1, Pallas kernels, on_device(): call(smooth_kernel, SMOOTH_OUTS, SMOOTH_SCRATCH)(main, after, before)  11.4 us
    pallas_call x1, Pallas kernels, on_device(): call(post_kernel, POST_OUTS, POST_SCRATCH)  9.16 us
    ppermute x5, waiting for transfers between devices, neighbours(): lax.ppermute(to_previous, axis, [(i + 1, i) for i in range(count - 1)])  6.22 us
  transfers between devices with their start and end apart: 10, of which 10 were waited for; matrix products, arithmetic and copies ran while one was open for 0% of the time, Pallas kernels for 0%

profile of v5, /device:TPU:302, one launch (start us, length us, event | category | flops | bytes accessed | tf_op | source)
XLA Modules:
  0.0 74.5 jit_solution(17499095764986320557)
XLA Ops:
  0.6 0.8 %fusion.2 = f32[1,8,8,128]{3,2,1,0:T(8,128)S(1)} fusion(s32[8,8,128]{2,1,0:T(8,128)} %param.2), kind=kLoop, calls=%fused_computation.4 | loop fusion | flops 57344 | bytes 65536 | tf_op jit(solution)/shard_map/broadcast_in_dim | solution.py:705
  1.4 0.9 %pad_maximum_fusion.own = f32[4,8,8,128]{3,2,1,0:T(8,128)S(1)} fusion(f32[1,8,8,128]{3,2,1,0:T(8,128)S(1)} %fusion.2, f32[3,8,8,128]{3,2,1,0:T(8,128)} %param.3), kind=kLoop, calls=%fused_computation | loop fusion | flops 32768 | bytes 262144 | tf_op jit(solution)/shard_map/concatenate | solution.py:705
  2.3 1.9 %collective-permute-start = (f32[25,8,128]{2,1,0:T(8,128)S(1)}, f32[25,8,128]{2,1,0:T(8,128)S(1)}, u32[]{:S(2)}, u32[]{:S(2)}) collective-permute-start(f32[25,8,128]{2,1,0:T(8,128)S(1)} %get-tuple-element.19), channel_id=1, source_target_pairs={{64,0},{128,64},{192,128},{256,192},{320,256},{384,320},{448,384},... | collective-permute-start | bytes 307208 | tf_op jit(solution)/shard_map/ppermute | solution.py:660
  4.3 3.9 %collective-permute-start.1 = (f32[25,8,128]{2,1,0:T(8,128)S(1)}, f32[25,8,128]{2,1,0:T(8,128)S(1)}, u32[]{:S(2)}, u32[]{:S(2)}) collective-permute-start(f32[25,8,128]{2,1,0:T(8,128)S(1)} %get-tuple-element.20), channel_id=1, source_target_pairs={{0,64},{64,128},{128,192},{192,256},{256,320},{320,384},{384,448},... | collective-permute-start | bytes 307208 | tf_op jit(solution)/shard_map/ppermute | solution.py:661
  8.2 0.7 collective-permute-done.right
  8.9 3.1 %collective-permute-done.1.left = f32[25,8,128]{2,1,0:T(8,128)S(1)} collective-permute-done((f32[25,8,128]{2,1,0:T(8,128)S(1)}, f32[25,8,128]{2,1,0:T(8,128)S(1)}, u32[]{:S(2)}, u32[]{:S(2)}) %collective-permute-start.1) | collective-permute-done | bytes 102432 | tf_op jit(solution)/shard_map/ppermute | solution.py:661
  12.1 3.3 %collective-permute-start.2 = (f32[520,128]{1,0:T(8,128)S(1)}, f32[520,128]{1,0:T(8,128)S(1)}, u32[]{:S(2)}, u32[]{:S(2)}) collective-permute-start(f32[520,128]{1,0:T(8,128)S(1)} %get-tuple-element.21), channel_id=1, source_target_pairs={{8,0},{16,8},{24,16},{32,24},{40,32},{48,40},{56,48},{9,1},{17,9},... | collective-permute-start | bytes 798728 | tf_op jit(solution)/shard_map/ppermute | solution.py:660
  15.4 2.6 %collective-permute-start.3 = (f32[520,128]{1,0:T(8,128)S(1)}, f32[520,128]{1,0:T(8,128)S(1)}, u32[]{:S(2)}, u32[]{:S(2)}) collective-permute-start(f32[520,128]{1,0:T(8,128)S(1)} %get-tuple-element.22), channel_id=1, source_target_pairs={{0,8},{8,16},{16,24},{24,32},{32,40},{40,48},{48,56},{1,9},{9,17},... | collective-permute-start | bytes 798728 | tf_op jit(solution)/shard_map/ppermute | solution.py:661
  18.0 3.0 %collective-permute-done.2.up = f32[520,128]{1,0:T(8,128)S(1)} collective-permute-done((f32[520,128]{1,0:T(8,128)S(1)}, f32[520,128]{1,0:T(8,128)S(1)}, u32[]{:S(2)}, u32[]{:S(2)}) %collective-permute-start.2) | collective-permute-done | bytes 266272 | tf_op jit(solution)/shard_map/ppermute | solution.py:660
  21.0 3.0 %collective-permute-done.3.down = f32[520,128]{1,0:T(8,128)S(1)} collective-permute-done((f32[520,128]{1,0:T(8,128)S(1)}, f32[520,128]{1,0:T(8,128)S(1)}, u32[]{:S(2)}, u32[]{:S(2)}) %collective-permute-start.3) | collective-permute-done | bytes 266272 | tf_op jit(solution)/shard_map/ppermute | solution.py:661
  24.0 0.8 %shard_map.43 = (f32[4,24,24,128]{3,2,1,0:T(8,128)S(1)}, f32[12,24,128]{2,1,0:T(8,128)S(1)}, f32[12,24,128]{2,1,0:T(8,128)S(1)}) custom-call(f32[4,8,8,128]{3,2,1,0:T(8,128)S(1)} %pad_maximum_fusion.own, f32[25,8,128]{2,1,0:T(8,128)S(1)} %collective-permute-done.right, f32[25,8,128]{2,1,0:T(8,128)S(1)} %collective-permute-done.1.left, ...), custom_call_target="tpu_custom_call" | custom-call | tf_op jit(solution)/shard_map/pallas_call | solution.py:710
  24.8 1.9 %collective-permute-start.4 = (f32[12,24,128]{2,1,0:T(8,128)S(1)}, f32[12,24,128]{2,1,0:T(8,128)S(1)}, u32[]{:S(2)}, u32[]{:S(2)}) collective-permute-start(f32[12,24,128]{2,1,0:T(8,128)S(1)} %get-tuple-element.24), channel_id=1, source_target_pairs={{1,0},{2,1},{3,2},{4,3},{5,4},{6,5},{7,6},{9,8},{10,9},{11,10},{12... | collective-permute-start | bytes 442376 | tf_op jit(solution)/shard_map/ppermute | solution.py:660
  26.7 2.4 %collective-permute-start.5 = (f32[12,24,128]{2,1,0:T(8,128)S(1)}, f32[12,24,128]{2,1,0:T(8,128)S(1)}, u32[]{:S(2)}, u32[]{:S(2)}) collective-permute-start(f32[12,24,128]{2,1,0:T(8,128)S(1)} %get-tuple-element.25), channel_id=1, source_target_pairs={{0,1},{1,2},{2,3},{3,4},{4,5},{5,6},{6,7},{8,9},{9,10},{10,11},{11... | collective-permute-start | bytes 442376 | tf_op jit(solution)/shard_map/ppermute | solution.py:661
  29.3 3.8 %collective-permute-done.5.before = f32[12,24,128]{2,1,0:T(8,128)S(1)} collective-permute-done((f32[12,24,128]{2,1,0:T(8,128)S(1)}, f32[12,24,128]{2,1,0:T(8,128)S(1)}, u32[]{:S(2)}, u32[]{:S(2)}) %collective-permute-start.5) | collective-permute-done | bytes 147488 | tf_op jit(solution)/shard_map/ppermute | solution.py:661
  33.2 11.4 %shard_map.44 = (f32[3,8,8,128]{3,2,1,0:T(8,128)S(1)}, f32[4,8,8,128]{3,2,1,0:T(8,128)S(1)}, f32[192,128]{1,0:T(8,128)S(1)}, f32[192,128]{1,0:T(8,128)S(1)}, f32...) custom-call(f32[4,24,24,128]{3,2,1,0:T(8,128)S(1)} %get-tuple-elemen, ...), custom_call_target="tpu_custom_call" | custom-call | tf_op jit(solution)/shard_map/pallas_call | solution.py:712
  44.6 1.9 %collective-permute-start.6 = (f32[192,128]{1,0:T(8,128)S(1)}, f32[192,128]{1,0:T(8,128)S(1)}, u32[]{:S(2)}, u32[]{:S(2)}) collective-permute-start(f32[192,128]{1,0:T(8,128)S(1)} %get-tuple-element.27), channel_id=1, source_target_pairs={{64,0},{128,64},{192,128},{256,192},{320,256},{384,320},{448,384},... | collective-permute-start | bytes 294920 | tf_op jit(solution)/shard_map/ppermute | solution.py:660
  46.5 3.9 %collective-permute-start.7 = (f32[192,128]{1,0:T(8,128)S(1)}, f32[192,128]{1,0:T(8,128)S(1)}, u32[]{:S(2)}, u32[]{:S(2)}) collective-permute-start(f32[192,128]{1,0:T(8,128)S(1)} %get-tuple-element.28), channel_id=1, source_target_pairs={{0,64},{64,128},{128,192},{192,256},{256,320},{320,384},{384,448},... | collective-permute-start | bytes 294920 | tf_op jit(solution)/shard_map/ppermute | solution.py:661
  50.5 0.7 collective-permute-done.6.right
  51.1 3.1 %collective-permute-done.7.left = f32[192,128]{1,0:T(8,128)S(1)} collective-permute-done((f32[192,128]{1,0:T(8,128)S(1)}, f32[192,128]{1,0:T(8,128)S(1)}, u32[]{:S(2)}, u32[]{:S(2)}) %collective-permute-start.7) | collective-permute-done | bytes 98336 | tf_op jit(solution)/shard_map/ppermute | solution.py:661
  54.3 3.6 %collective-permute-start.8 = (f32[368,128]{1,0:T(8,128)S(1)}, f32[368,128]{1,0:T(8,128)S(1)}, u32[]{:S(2)}, u32[]{:S(2)}) collective-permute-start(f32[368,128]{1,0:T(8,128)S(1)} %get-tuple-element.31), channel_id=1, source_target_pairs={{8,0},{16,8},{24,16},{32,24},{40,32},{48,40},{56,48},{9,1},{17,9},... | collective-permute-start | bytes 565256 | tf_op jit(solution)/shard_map/ppermute | solution.py:660
  57.9 2.3 %collective-permute-start.9 = (f32[368,128]{1,0:T(8,128)S(1)}, f32[368,128]{1,0:T(8,128)S(1)}, u32[]{:S(2)}, u32[]{:S(2)}) collective-permute-start(f32[368,128]{1,0:T(8,128)S(1)} %get-tuple-element.32), channel_id=1, source_target_pairs={{0,8},{8,16},{16,24},{24,32},{32,40},{40,48},{48,56},{1,9},{9,17},... | collective-permute-start | bytes 565256 | tf_op jit(solution)/shard_map/ppermute | solution.py:661
  60.2 1.6 %collective-permute-done.8.up = f32[368,128]{1,0:T(8,128)S(1)} collective-permute-done((f32[368,128]{1,0:T(8,128)S(1)}, f32[368,128]{1,0:T(8,128)S(1)}, u32[]{:S(2)}, u32[]{:S(2)}) %collective-permute-start.8) | collective-permute-done | bytes 188448 | tf_op jit(solution)/shard_map/ppermute | solution.py:660
  61.8 3.6 %collective-permute-done.9.down = f32[368,128]{1,0:T(8,128)S(1)} collective-permute-done((f32[368,128]{1,0:T(8,128)S(1)}, f32[368,128]{1,0:T(8,128)S(1)}, u32[]{:S(2)}, u32[]{:S(2)}) %collective-permute-start.9) | collective-permute-done | bytes 188448 | tf_op jit(solution)/shard_map/ppermute | solution.py:661
  65.4 9.2 %shard_map.46 = (f32[3,8,8,128]{3,2,1,0:T(8,128)}, f32[3,4,4,64]{3,2,1,0:T(4,128)}) custom-call(f32[4,8,8,128]{3,2,1,0:T(8,128)S(1)} %get-tuple-element.26.own, f32[192,128]{1,0:T(8,128)S(1)} %collective-permute-done.6.right, f32[192,128]{1,0:T(8,128)S(1)} %collective-permute-done.7.left, f32[368,128]{1,0:T(8,128)S(1)} %collective-permute-done.8.up, ...), custom_call_target="tpu_custom_call" | custom-call | tf_op jit(solution)/shard_map/pallas_call | solution.py:718
  (4 shorter events, 0.4 us)
Async XLA Ops:
  2.3 6.6 %collective-permute-start = (f32[25,8,128]{2,1,0:T(8,128)S(1)}, f32[25,8,128]{2,1,0:T(8,128)S(1)}, u32[]{:S(2)}, u32[]{:S(2)}) collective-permute-start(f32[25,8,128]{2,1,0:T(8,128)S(1)} %get-tuple-element.19), channel_id=1, source_target_pairs={{64,0},{128,64},{192,128},{256,192},{320,256},{384,320},{448,384},... | collective-permute-start | bytes 307208 | tf_op jit(solution)/shard_map/ppermute | solution.py:660
  4.3 7.8 %collective-permute-start.1 = (f32[25,8,128]{2,1,0:T(8,128)S(1)}, f32[25,8,128]{2,1,0:T(8,128)S(1)}, u32[]{:S(2)}, u32[]{:S(2)}) collective-permute-start(f32[25,8,128]{2,1,0:T(8,128)S(1)} %get-tuple-element.20), channel_id=1, source_target_pairs={{0,64},{64,128},{128,192},{192,256},{256,320},{320,384},{384,448},... | collective-permute-start | bytes 307208 | tf_op jit(solution)/shard_map/ppermute | solution.py:661
  12.1 8.9 %collective-permute-start.2 = (f32[520,128]{1,0:T(8,128)S(1)}, f32[520,128]{1,0:T(8,128)S(1)}, u32[]{:S(2)}, u32[]{:S(2)}) collective-permute-start(f32[520,128]{1,0:T(8,128)S(1)} %get-tuple-element.21), channel_id=1, source_target_pairs={{8,0},{16,8},{24,16},{32,24},{40,32},{48,40},{56,48},{9,1},{17,9},... | collective-permute-start | bytes 798728 | tf_op jit(solution)/shard_map/ppermute | solution.py:660
  15.4 8.6 %collective-permute-start.3 = (f32[520,128]{1,0:T(8,128)S(1)}, f32[520,128]{1,0:T(8,128)S(1)}, u32[]{:S(2)}, u32[]{:S(2)}) collective-permute-start(f32[520,128]{1,0:T(8,128)S(1)} %get-tuple-element.22), channel_id=1, source_target_pairs={{0,8},{8,16},{16,24},{24,32},{32,40},{40,48},{48,56},{1,9},{9,17},... | collective-permute-start | bytes 798728 | tf_op jit(solution)/shard_map/ppermute | solution.py:661
  24.8 4.6 %collective-permute-start.4 = (f32[12,24,128]{2,1,0:T(8,128)S(1)}, f32[12,24,128]{2,1,0:T(8,128)S(1)}, u32[]{:S(2)}, u32[]{:S(2)}) collective-permute-start(f32[12,24,128]{2,1,0:T(8,128)S(1)} %get-tuple-element.24), channel_id=1, source_target_pairs={{1,0},{2,1},{3,2},{4,3},{5,4},{6,5},{7,6},{9,8},{10,9},{11,10},{12... | collective-permute-start | bytes 442376 | tf_op jit(solution)/shard_map/ppermute | solution.py:660
  26.7 6.5 %collective-permute-start.5 = (f32[12,24,128]{2,1,0:T(8,128)S(1)}, f32[12,24,128]{2,1,0:T(8,128)S(1)}, u32[]{:S(2)}, u32[]{:S(2)}) collective-permute-start(f32[12,24,128]{2,1,0:T(8,128)S(1)} %get-tuple-element.25), channel_id=1, source_target_pairs={{0,1},{1,2},{2,3},{3,4},{4,5},{5,6},{6,7},{8,9},{9,10},{10,11},{11... | collective-permute-start | bytes 442376 | tf_op jit(solution)/shard_map/ppermute | solution.py:661
  44.6 6.5 %collective-permute-start.6 = (f32[192,128]{1,0:T(8,128)S(1)}, f32[192,128]{1,0:T(8,128)S(1)}, u32[]{:S(2)}, u32[]{:S(2)}) collective-permute-start(f32[192,128]{1,0:T(8,128)S(1)} %get-tuple-element.27), channel_id=1, source_target_pairs={{64,0},{128,64},{192,128},{256,192},{320,256},{384,320},{448,384},... | collective-permute-start | bytes 294920 | tf_op jit(solution)/shard_map/ppermute | solution.py:660
  46.5 7.7 %collective-permute-start.7 = (f32[192,128]{1,0:T(8,128)S(1)}, f32[192,128]{1,0:T(8,128)S(1)}, u32[]{:S(2)}, u32[]{:S(2)}) collective-permute-start(f32[192,128]{1,0:T(8,128)S(1)} %get-tuple-element.28), channel_id=1, source_target_pairs={{0,64},{64,128},{128,192},{192,256},{256,320},{320,384},{384,448},... | collective-permute-start | bytes 294920 | tf_op jit(solution)/shard_map/ppermute | solution.py:661
  54.3 7.5 %collective-permute-start.8 = (f32[368,128]{1,0:T(8,128)S(1)}, f32[368,128]{1,0:T(8,128)S(1)}, u32[]{:S(2)}, u32[]{:S(2)}) collective-permute-start(f32[368,128]{1,0:T(8,128)S(1)} %get-tuple-element.31), channel_id=1, source_target_pairs={{8,0},{16,8},{24,16},{32,24},{40,32},{48,40},{56,48},{9,1},{17,9},... | collective-permute-start | bytes 565256 | tf_op jit(solution)/shard_map/ppermute | solution.py:660
  57.9 7.5 %collective-permute-start.9 = (f32[368,128]{1,0:T(8,128)S(1)}, f32[368,128]{1,0:T(8,128)S(1)}, u32[]{:S(2)}, u32[]{:S(2)}) collective-permute-start(f32[368,128]{1,0:T(8,128)S(1)} %get-tuple-element.32), channel_id=1, source_target_pairs={{0,8},{8,16},{16,24},{24,32},{32,40},{40,48},{48,56},{1,9},{9,17},... | collective-permute-start | bytes 565256 | tf_op jit(solution)/shard_map/ppermute | solution.py:661
